TPU v7x, 128 devices: a whole 4x4x4 slice. The times are simulated.
128 devices in a mesh: fsdp: 4 (over y), ctx: 32 (over x, z, core).
Axes of the slice: x: 4, y: 4, z: 4, core: 2. Of those that a mesh axis runs over, the one named last changes fastest.
Arguments:
- hidden_in: bfloat16 [4, 4096, 576], P('fsdp', 'ctx'), may hold values from -6 to 6
- positions: int32 [4, 4096], P('fsdp', 'ctx'), may hold values from 0 to 4095, as said below
- params: bfloat16 [2, 6144, 576], P(None, ('fsdp', 'ctx')), may hold values from -3 to 3, as said below
- gains: bfloat16 [2, 1152], P(None, ('fsdp', 'ctx')), may hold values from 0.796875 to 1.1953125
- cotangent: bfloat16 [4, 4096, 576], P('fsdp', 'ctx'), may hold values from -6 to 6
Outputs:
- hidden_out: bfloat16 [4, 4096, 576], P('fsdp', 'ctx')
- grad_in: float32 [4, 4096, 576], P('fsdp', 'ctx')
- grad_params: float32 [2, 6144, 576], P(None, ('fsdp', 'ctx'))
- grad_gains: float32 [2, 1152], P(None, ('fsdp', 'ctx'))
Inputs may be any that keep to these rules, and one draw needn't show every extreme that they name: In each sequence every position of 0 to 4095 appears once; the 128 tokens of one device of ctx are the 64 consecutive positions of some block b and then those of block 63 - b, in order, b differing between devices. `params`: the layers' projection entries laid out as the steps state.
All inputs are finite; a program needn't handle non-finite values.
Results may differ from a plain program's by a relative error of at most 0.025.
Values may be sent and summed in bfloat16 or wider, within the bound.
A program may use at most 192 MiB of HBM per device.

v0:
```python
import jax
import jax.numpy as jnp
from jax import lax
from jax.sharding import PartitionSpec as P

MODEL_WIDTH = 576
FEEDFORWARD_SIZE = 1536
QUERY_HEADS = 9
KEY_VALUE_HEADS = 3
HEAD_SIZE = 64
LAYERS = 2


EPSILON = 1e-05
THETA = 100000.0
MASKED = -1e30
HIGHEST = lax.Precision.HIGHEST


def side_by_side(arrays, axis, dim, along):
    ends, at = ([], 0)
    for a in arrays[:-1]:
        at += a.shape[along]
        ends.append(at)
    both = jnp.concatenate(arrays, axis=along)
    return tuple(jnp.split(lax.all_gather(both, axis, axis=dim, tiled=True), ends, axis=along))


def in_one_piece(arrays, axis, dim, along):
    both = jnp.concatenate(arrays, axis=along)
    out, at, finished = (lax.psum_scatter(both, axis, scatter_dimension=dim, tiled=True), 0, [])
    for a in arrays:
        finished.append(lax.slice_in_dim(out, at, at + a.shape[along], axis=along))
        at += a.shape[along]
    return tuple(finished)


def copy_for_each(shard, axis):
    peers = lax.axis_size(axis)
    return lax.all_to_all(
        jnp.broadcast_to(shard[None], (peers, *shard.shape)), axis, 0, 0, tiled=True
    )


def laid_out(pieces, dim):
    pieces = jnp.moveaxis(pieces, 0, dim)
    lengths = pieces.shape
    return pieces.reshape(*lengths[:dim], lengths[dim] * lengths[dim + 1], *lengths[dim + 2 :])


def collect(shard, axis, dim):
    pieces = copy_for_each(shard, axis)
    return laid_out(pieces, dim)


def cut_along(shard, dim, peers):
    before, after = (shard.shape[:dim], shard.shape[dim + 1 :])
    return jnp.moveaxis(shard.reshape(*before, peers, -1, *after), dim, 0)


def sum_packed(arrays, axis, dims):
    peers = lax.axis_size(axis)
    pieces = [cut_along(a, dim, peers) for a, dim in zip(arrays, dims)]
    lines = jnp.concatenate([b.reshape(peers, -1) for b in pieces], axis=1)
    extent = max(16, -(-lines.shape[1] // 1024) * 8)
    lines = jnp.pad(lines, ((0, 0), (0, extent * 128 - lines.shape[1]))).reshape(-1, 128)
    flat, at, finished = (lax.psum_scatter(lines, axis, tiled=True).reshape(-1), 0, [])
    for b in pieces:
        part = b[0]
        finished.append(flat[at : at + part.size].reshape(part.shape))
        at += part.size
    return tuple(finished)


def unpack(weight_rows):
    row_counts = [
        QUERY_HEADS * HEAD_SIZE,
        KEY_VALUE_HEADS * HEAD_SIZE,
        KEY_VALUE_HEADS * HEAD_SIZE,
        QUERY_HEADS * HEAD_SIZE,
        FEEDFORWARD_SIZE,
        FEEDFORWARD_SIZE,
        FEEDFORWARD_SIZE,
    ]
    pieces = []
    offset = 0
    for amount in row_counts:
        pieces.append(weight_rows[offset : offset + amount])
        offset += amount
    return pieces


def rotation_parts(places, heads):
    feature_width = heads * HEAD_SIZE
    half_size = HEAD_SIZE // 2
    feature_index = jnp.arange(feature_width)
    within = feature_index % HEAD_SIZE
    pair_index = within % half_size
    frequency = 1.0 / THETA ** ((2 * pair_index).astype(jnp.float32) / HEAD_SIZE)
    phases = places.astype(jnp.float32)[:, None] * frequency[None, :]
    head_of = feature_index // HEAD_SIZE
    same_head = head_of[:, None] == head_of[None, :]
    lower_target = within[None, :] < half_size
    from_upper = (within[:, None] == within[None, :] + half_size) & lower_target
    from_lower = (within[:, None] + half_size == within[None, :]) & jnp.logical_not(lower_target)
    swapper = jnp.where(
        same_head & from_upper, -1.0, jnp.where(same_head & from_lower, 1.0, 0.0)
    ).astype(jnp.float32)
    return (jnp.cos(phases), jnp.sin(phases), swapper)


def apply_rotation(values, parts):
    cosine_wide, sine_wide, swapper = parts
    swapped = jnp.dot(values, swapper, precision=HIGHEST)
    return values * cosine_wide + swapped * sine_wide


def inverse_rotation(values, parts):
    cosine_wide, sine_wide, swapper = parts
    swapped = jnp.dot(values, swapper, precision=HIGHEST)
    return values * cosine_wide - swapped * sine_wide


def contract_rows(left_side, right_side):
    return lax.dot_general(
        left_side, right_side, (((0,), (0,)), ((), ())), preferred_element_type=jnp.float32
    )


def contract_cols(left_side, right_side):
    return lax.dot_general(
        left_side, right_side, (((1,), (1,)), ((), ())), preferred_element_type=jnp.float32
    )


def rms_inverse(values):
    return lax.rsqrt(jnp.mean(values * values, -1, keepdims=True) + EPSILON)


def norm_backward(grad_normed, values, inverse, gain):
    unit_rows = values * inverse
    grad_gain = jnp.sum(grad_normed * unit_rows, 0)
    scaled = grad_normed * gain.astype(jnp.float32)
    grad_values = inverse * (scaled - unit_rows * jnp.mean(scaled * unit_rows, -1, keepdims=True))
    return (grad_values, grad_gain)


def group_columns(rows, group, heads_here):
    width_here = heads_here * HEAD_SIZE
    piece = rows[:, group * width_here : (group + 1) * width_here]
    return piece.reshape(rows.shape[0], heads_here, HEAD_SIZE)


def masked_scores(query_group, key_group, allowed):
    scores = jnp.einsum(
        "tgd,kd->gtk", query_group, key_group, preferred_element_type=jnp.float32
    ) * HEAD_SIZE ** (-0.5)
    return jnp.where(allowed, scores, MASKED)


def attend_forward(query_rows, keys_all, values_all, allowed):
    count_of_rows = query_rows.shape[0]
    per_kv = QUERY_HEADS // KEY_VALUE_HEADS
    mixed_parts = []
    log_parts = []
    for group in range(KEY_VALUE_HEADS):
        query_group = group_columns(query_rows, group, per_kv)
        key_group = keys_all[:, group * HEAD_SIZE : (group + 1) * HEAD_SIZE]
        value_group = values_all[:, group * HEAD_SIZE : (group + 1) * HEAD_SIZE]
        scores = masked_scores(query_group, key_group, allowed)
        highest = jnp.max(scores, -1, keepdims=True)
        raised = jnp.exp(scores - highest)
        totals = jnp.sum(raised, -1, keepdims=True)
        weights = (raised / totals).astype(jnp.bfloat16)
        mixed = jnp.einsum("gtk,kd->tgd", weights, value_group, preferred_element_type=jnp.float32)
        mixed_parts.append(mixed.reshape(count_of_rows, per_kv * HEAD_SIZE))
        log_parts.append((highest + jnp.log(totals))[..., 0])
    return (jnp.concatenate(mixed_parts, -1), log_parts)


def attend_backward(query_rows, keys_all, values_all, grad_mixed, log_parts, allowed):
    count_of_rows = query_rows.shape[0]
    per_kv = QUERY_HEADS // KEY_VALUE_HEADS
    query_parts = []
    key_parts = []
    value_parts = []
    for group in range(KEY_VALUE_HEADS):
        query_group = group_columns(query_rows, group, per_kv)
        grad_group = group_columns(grad_mixed, group, per_kv)
        key_group = keys_all[:, group * HEAD_SIZE : (group + 1) * HEAD_SIZE]
        value_group = values_all[:, group * HEAD_SIZE : (group + 1) * HEAD_SIZE]
        scores = masked_scores(query_group, key_group, allowed)
        probabilities = jnp.exp(scores - log_parts[group][..., None])
        grad_probs = jnp.einsum(
            "tgd,kd->gtk", grad_group, value_group, preferred_element_type=jnp.float32
        )
        inner_sum = jnp.sum(grad_probs * probabilities, -1, keepdims=True)
        grad_scores = (probabilities * (grad_probs - inner_sum)).astype(jnp.bfloat16)
        grad_query = jnp.einsum(
            "gtk,kd->tgd", grad_scores, key_group, preferred_element_type=jnp.float32
        ) * HEAD_SIZE ** (-0.5)
        query_parts.append(grad_query.reshape(count_of_rows, per_kv * HEAD_SIZE))
        key_parts.append(
            jnp.einsum("gtk,tgd->kd", grad_scores, query_group, preferred_element_type=jnp.float32)
            * HEAD_SIZE ** (-0.5)
        )
        value_parts.append(
            jnp.einsum(
                "gtk,tgd->kd",
                probabilities.astype(jnp.bfloat16),
                grad_group,
                preferred_element_type=jnp.float32,
            )
        )
    return (
        jnp.concatenate(query_parts, -1),
        jnp.concatenate(key_parts, -1),
        jnp.concatenate(value_parts, -1),
    )


def layer_forward(hidden, weight_rows, gain_row, allowed, query_parts, key_parts):
    query_t, key_t, value_t, w_out, gate_t, up_t, w_down = unpack(weight_rows)
    gain_one = gain_row[:MODEL_WIDTH]
    gain_two = gain_row[MODEL_WIDTH:]
    inverse_one = rms_inverse(hidden)
    first_normalized = (hidden * inverse_one * gain_one.astype(jnp.float32)).astype(jnp.bfloat16)
    query_rows = apply_rotation(contract_cols(first_normalized, query_t), query_parts).astype(
        jnp.bfloat16
    )
    rows_of_keys = apply_rotation(contract_cols(first_normalized, key_t), key_parts).astype(
        jnp.bfloat16
    )
    rows_of_values = contract_cols(first_normalized, value_t).astype(jnp.bfloat16)
    keys_all, values_all = side_by_side((rows_of_keys, rows_of_values), "ctx", 0, 1)
    mixed, log_parts = attend_forward(query_rows, keys_all, values_all, allowed)
    mixed = mixed.astype(jnp.bfloat16)
    middle = hidden + jnp.dot(mixed, w_out, preferred_element_type=jnp.float32)
    inverse_two = rms_inverse(middle)
    normed_two = (middle * inverse_two * gain_two.astype(jnp.float32)).astype(jnp.bfloat16)
    gate_values = contract_cols(normed_two, gate_t)
    up_values = contract_cols(normed_two, up_t)
    product = (jax.nn.silu(gate_values) * up_values).astype(jnp.bfloat16)
    result = middle + jnp.dot(product, w_down, preferred_element_type=jnp.float32)
    kept_state = (
        hidden,
        inverse_one,
        first_normalized,
        query_rows,
        rows_of_keys,
        rows_of_values,
        mixed,
        log_parts,
        middle,
        inverse_two,
        normed_two,
        gate_values,
        up_values,
        product,
    )
    return (result, kept_state, (keys_all, values_all))


def layer_backward(
    grad_result,
    kept_state,
    weight_rows,
    gain_row,
    keys_all,
    values_all,
    allowed,
    query_parts,
    key_parts,
):
    (
        hidden,
        inverse_one,
        first_normalized,
        query_rows,
        rows_of_keys,
        rows_of_values,
        mixed,
        log_parts,
        middle,
        inverse_two,
        normed_two,
        gate_values,
        up_values,
        product,
    ) = kept_state
    query_t, key_t, value_t, w_out, gate_t, up_t, w_down = unpack(weight_rows)
    gain_one = gain_row[:MODEL_WIDTH]
    gain_two = gain_row[MODEL_WIDTH:]
    grad_down = grad_result.astype(jnp.bfloat16)
    grad_w_down = contract_rows(product, grad_down)
    grad_product = contract_cols(grad_down, w_down)
    sigmoid_values = jax.nn.sigmoid(gate_values)
    grad_gate = (
        grad_product * up_values * (sigmoid_values * (1.0 + gate_values * (1.0 - sigmoid_values)))
    ).astype(jnp.bfloat16)
    grad_up = (grad_product * (gate_values * sigmoid_values)).astype(jnp.bfloat16)
    grad_gate_t = contract_rows(grad_gate, normed_two)
    grad_up_t = contract_rows(grad_up, normed_two)
    grad_normed_two = jnp.dot(grad_gate, gate_t, preferred_element_type=jnp.float32) + jnp.dot(
        grad_up, up_t, preferred_element_type=jnp.float32
    )
    grad_middle, grad_gain_two = norm_backward(grad_normed_two, middle, inverse_two, gain_two)
    grad_middle = grad_middle + grad_result
    grad_branch = grad_middle.astype(jnp.bfloat16)
    grad_w_out = contract_rows(mixed, grad_branch)
    grad_mixed = contract_cols(grad_branch, w_out).astype(jnp.bfloat16)
    grad_query, key_terms, value_terms = attend_backward(
        query_rows, keys_all, values_all, grad_mixed, log_parts, allowed
    )
    key_sums, value_sums = tuple(
        (
            part.astype(jnp.float32)
            for part in in_one_piece(
                (key_terms.astype(jnp.bfloat16), value_terms.astype(jnp.bfloat16)), "ctx", 0, 1
            )
        )
    )
    grad_query = inverse_rotation(grad_query, query_parts).astype(jnp.bfloat16)
    key_gradient = inverse_rotation(key_sums, key_parts).astype(jnp.bfloat16)
    value_gradient = value_sums.astype(jnp.bfloat16)
    grad_query_t = contract_rows(grad_query, first_normalized)
    grad_key_t = contract_rows(key_gradient, first_normalized)
    grad_value_t = contract_rows(value_gradient, first_normalized)
    grad_normed_one = (
        jnp.dot(grad_query, query_t, preferred_element_type=jnp.float32)
        + jnp.dot(key_gradient, key_t, preferred_element_type=jnp.float32)
        + jnp.dot(value_gradient, value_t, preferred_element_type=jnp.float32)
    )
    grad_hidden, grad_gain_one = norm_backward(grad_normed_one, hidden, inverse_one, gain_one)
    grad_hidden = grad_hidden + grad_middle
    grad_rows = jnp.concatenate(
        [grad_query_t, grad_key_t, grad_value_t, grad_w_out, grad_gate_t, grad_up_t, grad_w_down], 0
    )
    grad_gain_row = jnp.concatenate([grad_gain_one, grad_gain_two])
    return (grad_hidden, grad_rows, grad_gain_row)


def on_device(hidden_in, positions, params, gains, cotangent):
    own_places = positions[0]
    key_places = collect(own_places, "ctx", 0)
    allowed = key_places[None, None, :] <= own_places[None, :, None]
    query_parts = rotation_parts(own_places, QUERY_HEADS)
    key_parts = rotation_parts(own_places, KEY_VALUE_HEADS)
    hidden = hidden_in[0].astype(jnp.float32)
    kept_states = []
    kept_weights = []
    kept_gathered = []
    for layer_index in range(LAYERS):
        weight_rows, gain_row = (
            lax.all_gather(params[layer_index], ("fsdp", "ctx"), axis=0, tiled=True),
            lax.all_gather(gains[layer_index], ("fsdp", "ctx"), axis=0, tiled=True),
        )
        hidden, kept_state, gathered = layer_forward(
            hidden, weight_rows, gain_row, allowed, query_parts, key_parts
        )
        kept_states.append(kept_state)
        kept_weights.append((weight_rows, gain_row))
        kept_gathered.append(gathered)
    output_rows = hidden.astype(jnp.bfloat16)
    grad_hidden = cotangent[0].astype(jnp.float32)
    grad_row_shards = [None] * LAYERS
    grad_gain_shards = [None] * LAYERS
    for layer_index in reversed(range(LAYERS)):
        kept_state = kept_states[layer_index]
        weight_rows, gain_row = kept_weights[layer_index]
        keys_all, values_all = kept_gathered[layer_index]
        grad_hidden, grad_rows, grad_gain_row = layer_backward(
            grad_hidden,
            kept_state,
            weight_rows,
            gain_row,
            keys_all,
            values_all,
            allowed,
            query_parts,
            key_parts,
        )
        group_rows, group_gains = (
            lax.psum_scatter(
                grad_rows.astype(jnp.bfloat16), "fsdp", scatter_dimension=0, tiled=True
            ).astype(jnp.float32),
            lax.psum_scatter(
                grad_gain_row.astype(jnp.bfloat16), "fsdp", scatter_dimension=0, tiled=True
            ).astype(jnp.float32),
        )
        owned_rows, owned_gains = tuple(
            (
                part.astype(jnp.float32)
                for part in sum_packed(
                    (group_rows.astype(jnp.bfloat16), group_gains.astype(jnp.bfloat16)),
                    "ctx",
                    (0, 0),
                )
            )
        )
        grad_row_shards[layer_index] = owned_rows
        grad_gain_shards[layer_index] = owned_gains
    return (
        output_rows[None],
        grad_hidden[None],
        jnp.stack(grad_row_shards),
        jnp.stack(grad_gain_shards),
    )


def solution(mesh):
    return jax.shard_map(
        on_device,
        mesh=mesh,
        in_specs=(
            P("fsdp", "ctx", None),
            P("fsdp", "ctx"),
            P(None, ("fsdp", "ctx"), None),
            P(None, ("fsdp", "ctx")),
            P("fsdp", "ctx", None),
        ),
        out_specs=(
            P("fsdp", "ctx", None),
            P("fsdp", "ctx", None),
            P(None, ("fsdp", "ctx"), None),
            P(None, ("fsdp", "ctx")),
        ),
        check_vma=False,
    )
```

profile of v0, /device:TPU:1, one launch (start us, length us, event | category | flops | bytes accessed | tf_op | source)
XLA Modules:
  0.0 870.5 jit_solution(2909045545491602982)
XLA Ops:
  10.0 69.4 %all-reduce.6 = (bf16[1152]{0:T(1024)(128)(2,1)S(1)}, bf16[1152]{0:T(1024)(128)(2,1)S(1)}) all-reduce(bf16[1152]{0:T(1024)(128)(2,1)S(1)} %dynamic-update-slice, bf16[1152]{0:T(1024)(128)(2,1)S(1)} %dynamic-update-slice.1), channel_id=2, replica_groups=mesh['fsdp'=4,'ctx'=32] {'fsdp','ctx'}, use_global_device_ids=true, to_apply=%add.2 | all-reduce | flops 2304 | bytes 9216
  81.2 4.1 all-gather.13.cloned.1.call-done
  91.5 4.5 all-to-all-start
  96.3 6.7 all-to-all-done
  110.9 22.9 %all-gather.9.cloned.1.call-done = bf16[4096,384]{0,1:T(8,128)(2,1)} async-done(((bf16[128,384]{0,1:T(8,128)(2,1)}), bf16[4096,384]{0,1:T(8,128)(2,1)}) %all-gather.9.cloned.1.call-update) | async-done | bytes 3145744 | tf_op jit(solution)/shard_map/all_gather | solution.py:26
  154.4 52.0 %all-gather.15.cloned.1.call-done = bf16[1,6144,576]{2,1,0:T(8,128)(2,1)} async-done(((bf16[1,48,576]{2,1,0:T(8,128)(2,1)}), bf16[1,6144,576]{2,1,0:T(8,128)(2,1)}) %all-gather.15.cloned.1.call-update) | async-done | bytes 7077904 | tf_op jit(solution)/shard_map/all_gather | solution.py:355
  215.4 39.5 %all-gather.11.cloned.1.call-done = bf16[4096,384]{0,1:T(8,128)(2,1)} async-done(((bf16[128,384]{0,1:T(8,128)(2,1)}), bf16[4096,384]{0,1:T(8,128)(2,1)}) %all-gather.11.cloned.1.call-update) | async-done | bytes 3145744 | tf_op jit(solution)/shard_map/all_gather | solution.py:26
  275.4 3.9 fusion.15
  279.3 5.9 fusion.17
  289.0 5.0 fusion.9
  294.0 6.0 fusion.11
  300.0 5.4 fusion.12
  305.3 5.9 fusion.14
  311.3 4.0 fusion.46
  323.0 4.8 copy.121
  339.1 66.7 %reduce-scatter.19.cloned.1.call-done = bf16[128,384]{1,0:T(8,128)(2,1)} async-done(((bf16[4096,384]{1,0:T(8,128)(2,1)}), bf16[128,384]{1,0:T(8,128)(2,1)}) %reduce-scatter.19.cloned.1.call-update) | async-done | bytes 98320
  422.4 4.9 fusion.6
  427.4 4.6 fusion.8
  433.9 5.0 fusion
  438.9 6.1 fusion.2
  445.0 5.0 fusion.3
  450.0 6.0 fusion.5
  455.9 4.0 fusion.43
  467.7 4.8 copy.123
  485.9 11.1 %concatenate.69 = bf16[6144,576]{0,1:T(8,128)(2,1)} concatenate(bf16[576,576]{0,1:T(8,128)(2,1)} %convolution_convert_fusion.7, bf16[192,576]{0,1:T(8,128)(2,1)} %copy.94, bf16[192,576]{0,1:T(8,128)(2,1)} %copy.95, bf16[576,576]{0,1:T(8,128)(2,1)} %convolution_convert_fusion.6, bf16[1536,576]{0,1:T(8,128)(2,1)S(1)} %convolution_convert_fusion.2, ...), dimensions={0} | concatenate | bytes 14155776 | tf_op jit(solution)/shard_map/concatenate | solution.py:336
  513.9 38.5 %reduce-scatter.21.cloned.1.call-done = bf16[128,384]{1,0:T(8,128)(2,1)} async-done(((bf16[4096,384]{1,0:T(8,128)(2,1)}), bf16[128,384]{1,0:T(8,128)(2,1)}) %reduce-scatter.21.cloned.1.call-update) | async-done | bytes 98320
  565.3 11.1 %concatenate.66 = bf16[6144,576]{0,1:T(8,128)(2,1)} concatenate(bf16[576,576]{0,1:T(8,128)(2,1)} %convolution_convert_fusion.9, bf16[192,576]{0,1:T(8,128)(2,1)} %copy.91, bf16[192,576]{0,1:T(8,128)(2,1)} %copy.92, bf16[576,576]{0,1:T(8,128)(2,1)} %convolution_convert_fusion.8, bf16[1536,576]{0,1:T(8,128)(2,1)S(1)} %convolution_convert_fusion.5, ...), dimensions={0} | concatenate | bytes 14155776 | tf_op jit(solution)/shard_map/concatenate | solution.py:336
  582.8 10.0 %all-reduce.7 = (bf16[1152]{0:T(1024)(128)(2,1)S(1)}, bf16[1152]{0:T(1024)(128)(2,1)S(1)}) all-reduce(bf16[1152]{0:T(1024)(128)(2,1)S(1)} %pad_maximum_fusion.9, bf16[1152]{0:T(1024)(128)(2,1)S(1)} %pad_maximum_fusion.8), channel_id=12, replica_groups=mesh['fsdp'=4,'ctx'=32] {'fsdp'}, use_global_device_ids=true, to_apply=%region_36.37.clone | all-reduce | flops 2304 | bytes 9216
  593.2 33.3 %reduce-scatter.15.cloned.1.call-done = bf16[1536,576]{0,1:T(8,128)(2,1)} async-done(((bf16[6144,576]{0,1:T(8,128)(2,1)}), bf16[1536,576]{0,1:T(8,128)(2,1)}) %reduce-scatter.15.cloned.1.call-update) | async-done | bytes 1769488 | tf_op jit(solution)/shard_map/reduce_scatter | solution.py:384
  635.5 63.4 %reduce-scatter.11.cloned.1.call-done = bf16[1536,576]{0,1:T(8,128)(2,1)} async-done(((bf16[6144,576]{0,1:T(8,128)(2,1)}), bf16[1536,576]{0,1:T(8,128)(2,1)}) %reduce-scatter.11.cloned.1.call-update) | async-done | bytes 1769488 | tf_op jit(solution)/shard_map/reduce_scatter | solution.py:384
  711.9 67.3 %reduce-scatter.17.cloned.1.call-done = bf16[224,128]{1,0:T(8,128)(2,1)} async-done(((bf16[7168,128]{1,0:T(8,128)(2,1)}), bf16[224,128]{1,0:T(8,128)(2,1)}) %reduce-scatter.17.cloned.1.call-update) | async-done | bytes 57360 | tf_op jit(solution)/shard_map/reduce_scatter | solution.py:67
  780.8 79.7 %reduce-scatter.13.cloned.1.call-done = bf16[224,128]{1,0:T(8,128)(2,1)} async-done(((bf16[7168,128]{1,0:T(8,128)(2,1)}), bf16[224,128]{1,0:T(8,128)(2,1)}) %reduce-scatter.13.cloned.1.call-update) | async-done | bytes 57360 | tf_op jit(solution)/shard_map/reduce_scatter | solution.py:67
  (487 shorter events, 191.5 us)
Async XLA Ops:
  7.2 78.2 %all-gather.13.cloned.1.call-start = ((), (), s32[]{:S(2)}) async-start(), calls=%async_computation.13 | async-start | bytes 7925760 | tf_op jit(solution)/shard_map/all_gather | solution.py:355
  8.7 125.1 %all-gather.9.cloned.1.call-start = ((), (), s32[]{:S(2)}) async-start(), calls=%async_computation.7 | async-start | bytes 3244032 | tf_op jit(solution)/shard_map/all_gather | solution.py:26
  79.4 128.3 %copy-start.128 = (f32[192]{0:T(256)}, f32[192]{0:T(256)S(1)}, u32[]{:S(2)}) copy-start(f32[192]{0:T(256)S(1)} %fusion.232) | copy-start | bytes 2308
  79.4 128.3 %copy-start.130 = (s32[192]{0:T(256)}, s32[192]{0:T(256)S(1)}, u32[]{:S(2)}) copy-start(s32[192]{0:T(256)S(1)} %broadcast_add_fusion.1) | copy-start | bytes 2308
  79.4 128.2 %copy-start.132 = (pred[192]{0:T(512)(128)(4,1)}, pred[192]{0:T(512)(128)(4,1)S(1)}, u32[]{:S(2)}) copy-start(pred[192]{0:T(512)(128)(4,1)S(1)} %get-tuple-element.83) | copy-start | bytes 580
  79.4 128.2 %copy-start.134 = (pred[192]{0:T(512)(128)(4,1)}, pred[192]{0:T(512)(128)(4,1)S(1)}, u32[]{:S(2)}) copy-start(pred[192]{0:T(512)(128)(4,1)S(1)} %get-tuple-element.84) | copy-start | bytes 580
  79.4 128.2 %copy-start.115 = (s32[192]{0:T(256)}, s32[192]{0:T(256)S(1)}, u32[]{:S(2)}) copy-start(s32[192]{0:T(256)S(1)} %get-tuple-element.81) | copy-start | bytes 2308
  79.4 128.2 %copy-start.118 = (s32[192]{0:T(256)}, s32[192]{0:T(256)S(1)}, u32[]{:S(2)}) copy-start(s32[192]{0:T(256)S(1)} %get-tuple-element.82) | copy-start | bytes 2308
  81.2 130.6 %copy-start.136 = (f32[128]{0:T(128)}, f32[128]{0:T(128)S(1)}, u32[]{:S(2)}) copy-start(f32[128]{0:T(128)S(1)} %bitcast_convert_fusion) | copy-start | bytes 1540
  89.5 116.9 %all-gather.15.cloned.1.call-start = ((), (), s32[]{:S(2)}) async-start(), calls=%async_computation.14 | async-start | bytes 7925760 | tf_op jit(solution)/shard_map/all_gather | solution.py:355
  91.5 11.4 %all-to-all-start = ((s32[32,1,128]{2,1,0:T(1,128)}), s32[32,1,128]{2,1,0:T(1,128)S(1)}, u32[]{:S(2)}, u32[]{:S(2)}) async-start(s32[32,1,128]{2,1,0:T(1,128)} %broadcast_in_dim.146), calls=%async_computation | async-start | bytes 32768 | tf_op jit(solution)/shard_map/all_to_all | solution.py:40
  96.0 158.9 %all-gather.11.cloned.1.call-start = ((), (), s32[]{:S(2)}) async-start(), calls=%async_computation.8 | async-start | bytes 3244032 | tf_op jit(solution)/shard_map/all_gather | solution.py:26
  96.1 115.7 %copy-start.99 = (f32[576]{0:T(1024)}, f32[576]{0:T(1024)S(1)}, u32[]{:S(2)}) copy-start(f32[576]{0:T(1024)S(1)} %fusion.217) | copy-start | bytes 6916
  96.1 115.7 %copy-start.102 = (s32[576]{0:T(1024)}, s32[576]{0:T(1024)S(1)}, u32[]{:S(2)}) copy-start(s32[576]{0:T(1024)S(1)} %broadcast_add_fusion) | copy-start | bytes 6916
  96.1 115.7 %copy-start.105 = (s32[576]{0:T(1024)}, s32[576]{0:T(1024)S(1)}, u32[]{:S(2)}) copy-start(s32[576]{0:T(1024)S(1)} %get-tuple-element.77) | copy-start | bytes 6916
  96.2 115.7 %copy-start.108 = (s32[576]{0:T(1024)}, s32[576]{0:T(1024)S(1)}, u32[]{:S(2)}) copy-start(s32[576]{0:T(1024)S(1)} %get-tuple-element.78) | copy-start | bytes 6916
  96.3 115.6 %copy-start.121 = (pred[576]{0:T(1024)(128)(4,1)}, pred[576]{0:T(1024)(128)(4,1)S(1)}, u32[]{:S(2)}) copy-start(pred[576]{0:T(1024)(128)(4,1)S(1)} %get-tuple-element.79) | copy-start | bytes 1732
  96.3 115.6 %copy-start.124 = (pred[576]{0:T(1024)(128)(4,1)}, pred[576]{0:T(1024)(128)(4,1)S(1)}, u32[]{:S(2)}) copy-start(pred[576]{0:T(1024)(128)(4,1)S(1)} %get-tuple-element.80) | copy-start | bytes 1732
  105.7 152.4 %copy-start.43 = (pred[128,4096]{0,1:T(8,128)(4,1)}, pred[128,4096]{0,1:T(8,128)(4,1)S(1)}, u32[]{:S(2)}) copy-start(pred[128,4096]{0,1:T(8,128)(4,1)S(1)} %broadcast_compare_fusion) | copy-start | bytes 1572868
  154.4 318.3 %copy-start.14 = (bf16[128,576]{0,1:T(8,128)(2,1)}, bf16[128,576]{0,1:T(8,128)(2,1)S(1)}, u32[]{:S(2)}) copy-start(bf16[128,576]{0,1:T(8,128)(2,1)S(1)} %multiply_convert_fusion.7) | copy-start | bytes 442372
  210.3 195.6 %reduce-scatter.19.cloned.1.call-start = ((), (), s32[]{:S(2)}) async-start(), calls=%async_computation.15 | async-start | bytes 3244032
  268.8 206.4 %copy-start.13 = (bf16[128,576]{0,1:T(8,128)(2,1)}, bf16[128,576]{0,1:T(8,128)(2,1)S(1)}, u32[]{:S(2)}) copy-start(bf16[128,576]{0,1:T(8,128)(2,1)S(1)} %multiply_convert_fusion.6) | copy-start | bytes 442372
  327.8 224.6 %reduce-scatter.21.cloned.1.call-start = ((), (), s32[]{:S(2)}) async-start(), calls=%async_computation.16 | async-start | bytes 3244032
  333.8 73.0 %copy-start.116 = (s32[192]{0:T(256)S(1)}, s32[192]{0:T(256)}, u32[]{:S(2)}) copy-start(s32[192]{0:T(256)} %copy-done.115) | copy-start | bytes 2308
  334.0 75.7 %copy-start.28 = (f32[128,576]{0,1:T(8,128)S(1)}, f32[128,576]{0,1:T(8,128)}, u32[]{:S(2)}) copy-start(f32[128,576]{0,1:T(8,128)} %copy-done.26) | copy-start | bytes 884740
  334.0 75.7 %copy-start.98 = (f32[128]{0:T(128)S(1)}, f32[128]{0:T(128)}, u32[]{:S(2)}) copy-start(f32[128]{0:T(128)} %copy-done.97) | copy-start | bytes 1540
  334.0 77.8 %copy-start.24 = (f32[128,576]{0,1:T(8,128)S(1)}, f32[128,576]{0,1:T(8,128)}, u32[]{:S(2)}) copy-start(f32[128,576]{0,1:T(8,128)} %copy-done.23) | copy-start | bytes 884740
  337.5 74.5 %copy-start.36 = (f32[128,1536]{1,0:T(8,128)S(1)}, f32[128,1536]{1,0:T(8,128)}, u32[]{:S(2)}) copy-start(f32[128,1536]{1,0:T(8,128)} %copy-done.35) | copy-start | bytes 2359300
  472.4 154.1 %reduce-scatter.15.cloned.1.call-start = ((), (), s32[]{:S(2)}) async-start(), calls=%async_computation.11 | async-start | bytes 8847360 | tf_op jit(solution)/shard_map/reduce_scatter | solution.py:384
  497.1 201.8 %reduce-scatter.11.cloned.1.call-start = ((), (), s32[]{:S(2)}) async-start(), calls=%async_computation.9 | async-start | bytes 8847360 | tf_op jit(solution)/shard_map/reduce_scatter | solution.py:384
  576.5 202.7 %reduce-scatter.17.cloned.1.call-start = ((), (), s32[]{:S(2)}) async-start(), calls=%async_computation.12 | async-start | bytes 1892352 | tf_op jit(solution)/shard_map/reduce_scatter | solution.py:67
  635.4 225.1 %reduce-scatter.13.cloned.1.call-start = ((), (), s32[]{:S(2)}) async-start(), calls=%async_computation.10 | async-start | bytes 1892352 | tf_op jit(solution)/shard_map/reduce_scatter | solution.py:67
  (128 other events, 1293.9 us)
Sparse Core Ops, SparseCore 0:
  11.6 73.7 all-gather.12
  89.7 44.1 all-gather.8
  137.5 68.9 all-gather.14
  210.4 44.4 all-gather.10
  327.9 77.8 reduce-scatter.18
  472.6 79.7 reduce-scatter.20
  554.8 71.6 reduce-scatter.14
  628.9 69.9 reduce-scatter.10
  702.5 76.7 reduce-scatter.16
  782.6 77.8 reduce-scatter.12
where the time goes:
time: 878 us; the launch traced here: 871 us
  waiting for transfers between devices  475 us (54%)
  matrix products  166 us (19%)
  blocking collectives  79.4 us (9%)
  local copies, waits for them, and re-layouts  74.9 us (9%)
  other arithmetic  52.5 us (6%)
  between operations  17.5 us (2%)
    reduce_scatter x2, waiting for transfers between devices, sum_packed(): lax.psum_scatter(lines, axis, tiled=True).reshape(-1)  147 us
    unnamed x12, waiting for transfers between devices  106 us
    reduce_scatter x2, waiting for transfers between devices, on_device(): lax.psum_scatter(grad_rows.astype(jnp.bfloat16), 'fsdp', scatter_dimensio...  96.7 us
    unnamed x2, blocking collectives  79.4 us
    all_gather x2, waiting for transfers between devices, side_by_side(): lax.all_gather(both, axis, axis=dim, tiled=True)  62.4 us
    all_gather x2, waiting for transfers between devices, on_device(): lax.all_gather(params[layer_index], ('fsdp', 'ctx'), axis=0, tiled=True)  56.1 us
    convert_element_type x6, other arithmetic, attend_backward(): (probabilities * (grad_probs - inner_sum)).astype(jnp.bfloat16)  34.6 us
    dot_general x6, matrix products, attend_backward(): jnp.einsum('tgd,kd->gtk', grad_group, value_group, preferred_element_type...  29.1 us
  transfers between devices with their start and end apart: 11, of which 11 were waited for; matrix products, arithmetic and copies ran while one was open for 16% of the time, Pallas kernels for 0%

commit v1 on v0

v1 whole, which is shorter than its diff:
```python
import functools

import jax
import jax.numpy as jnp
from jax import lax
from jax.experimental import pallas as pl
from jax.experimental.pallas import tpu as pltpu
from jax.sharding import PartitionSpec as P

MODEL_WIDTH = 576
FEEDFORWARD_SIZE = 1536
QUERY_HEADS = 9
KEY_VALUE_HEADS = 3
HEAD_SIZE = 64
LAYERS = 2
KV_WIDTH = 2 * KEY_VALUE_HEADS * HEAD_SIZE

EPSILON = 1e-05
THETA = 100000.0
MASKED = -1e30
HIGHEST = lax.Precision.HIGHEST
MESH = pl.DeviceIdType.MESH
RING = 4


def place():
    t = lax.axis_index("ctx")
    return (lax.axis_index("fsdp"), t // 8, (t // 2) % 4, t % 2)


def device(y, x, z, c):
    return (y, x * 8 + z * 2 + c)


def moved(me, axis, step):
    other = list(me)
    other[axis] = (me[axis] + step) % RING
    return tuple(other)


def sibling(me):
    return (me[0], me[1], me[2], 1 - me[3])


def greet(peers):
    barrier = pltpu.get_barrier_semaphore()
    for peer in peers:
        pl.semaphore_signal(barrier, inc=1, device_id=device(*peer), device_id_type=MESH)
    pl.semaphore_wait(barrier, len(peers))


TILES = 33
CHUNK = 11
LANES = 384


def head_lanes():
    return lax.broadcasted_iota(jnp.int32, (1, LANES), 1) % 128 >= 64


def roll_heads(rows):
    return jnp.concatenate(
        [pltpu.roll(rows[:, 128 * h : 128 * h + 128], 64, 1) for h in range(3)], axis=1
    )


def pack_tile(lo, hi, keep_lo, use_a, use_b):
    lo = lo.astype(jnp.float32)
    hi = hi.astype(jnp.float32)
    zero = jnp.zeros_like(lo)
    a = jnp.where(use_a, lo, zero)
    b = jnp.where(use_b, hi, zero)
    if not keep_lo:
        lo = zero
    left = lax.broadcasted_iota(jnp.int32, (64, 128), 1) < 64
    keys = [jnp.where(left, lo, pltpu.roll(a, 64, 1)), jnp.where(left, b, zero)]
    values = [jnp.where(left, pltpu.roll(lo, 64, 1), a), jnp.where(left, pltpu.roll(b, 64, 1), zero)]
    return (
        jnp.concatenate(keys, axis=1).astype(jnp.bfloat16),
        jnp.concatenate(values, axis=1).astype(jnp.bfloat16),
    )


def pack_all(g, kv, own, tall, keys, values):
    def one(t, carry):
        at = kv[g, t // 8, (t // 2) % 4, t % 2]
        use_a = jnp.broadcast_to(tall[t][:1] > 0.5, (64, 128))
        k, v = pack_tile(at[:64], at[64:], True, use_a, jnp.logical_not(use_a))
        spot = pl.ds(pl.multiple_of(t * 64, 64), 64)
        keys[spot] = k
        values[spot] = v
        return carry

    lax.fori_loop(0, TILES - 1, one, 0)
    yes = jnp.full((64, 128), True)
    k, v = pack_tile(own[g, :64], own[g, 64:], False, yes, jnp.logical_not(yes))
    keys[pl.ds(64 * (TILES - 1), 64)] = k
    values[pl.ds(64 * (TILES - 1), 64)] = v


def dot_cols(left, right):
    return lax.dot_general(
        left, right, (((1,), (1,)), ((), ())), preferred_element_type=jnp.float32
    )


def dot_rows(left, right):
    return lax.dot_general(
        left, right, (((0,), (0,)), ((), ())), preferred_element_type=jnp.float32
    )


def score_all(keys, queries, scores):
    for c in range(TILES // CHUNK):
        rows = pl.ds(64 * CHUNK * c, 64 * CHUNK)
        scores[rows] = dot_cols(keys[rows], queries)
    at = lax.broadcasted_iota(jnp.int32, (64, LANES), 0)
    lane = lax.broadcasted_iota(jnp.int32, (64, LANES), 1) % 128
    causal = jnp.logical_and(lane < 64, at <= lane)
    mine = pl.ds(pl.multiple_of(lax.axis_index("ctx") * 64, 64), 64)
    scores[mine] = jnp.where(jnp.logical_or(lane >= 64, causal), scores[mine], MASKED)
    last = pl.ds(64 * (TILES - 1), 64)
    scores[last] = jnp.where(causal, scores[last], MASKED)


def tile_rows(flags, row):
    crossed = jnp.where(head_lanes(), row, roll_heads(row))
    return jnp.where(flags[...] > 0.5, row, crossed)


def joined(rows, flags, merge, empty):
    straight = jnp.where(jnp.logical_or(head_lanes(), flags[...] > 0.5), rows, empty)
    crossed = jnp.where(jnp.logical_or(head_lanes(), flags[...] > 0.5), empty, rows)
    down = jnp.max if merge is jnp.maximum else jnp.sum
    one = down(straight, axis=0, keepdims=True)
    other = roll_heads(down(crossed, axis=0, keepdims=True))
    return merge(one, other)


def fold_lanes(product):
    return jnp.where(
        head_lanes(), product[:64] + roll_heads(product[128:192]), product[64:128]
    )


def attend_group(g, own, kv, queries, flags, tall, out, lse, keys, values, scores, rows):
    pack_all(g, kv, own, tall, keys, values)
    score_all(keys, queries[g], scores)
    rows[...] = jnp.full(rows.shape, MASKED, jnp.float32)

    for t in range(TILES):
        rows[pl.ds(t, 1)] = jnp.max(scores[pl.ds(64 * t, 64)], axis=0, keepdims=True)
    top = joined(rows[...], flags, jnp.maximum, MASKED)
    rows[...] = tile_rows(flags, top)
    total = jnp.zeros((256, LANES), jnp.float32)
    sums = []
    for c in range(TILES // CHUNK):
        parts = []
        for i in range(CHUNK):
            t = c * CHUNK + i
            raised = jnp.exp(scores[pl.ds(64 * t, 64)] - rows[pl.ds(t, 1)])
            sums.append(jnp.sum(raised, axis=0, keepdims=True))
            parts.append(raised.astype(jnp.bfloat16))
        spot = pl.ds(64 * CHUNK * c, 64 * CHUNK)
        total = total + dot_rows(values[spot], jnp.concatenate(parts, axis=0))
    rows[...] = jnp.zeros(rows.shape, jnp.float32)
    for t in range(TILES):
        rows[pl.ds(t, 1)] = sums[t]
    amount = joined(rows[...], flags, jnp.add, 0.0)
    out[g] = fold_lanes(total) / amount
    lse[g] = jnp.broadcast_to(top + jnp.log(amount), (8, LANES))


def attend_back_group(
    g, me, kv, own, queries, grads, lse, inner, flags, tall, dq, dkv,
    keys, values, scores, lse_rows, inner_rows,
):
    pack_all(g, kv, own, tall, keys, values)
    score_all(keys, queries[g], scores)
    lse_rows[...] = tile_rows(flags, lse[g][:1])
    inner_rows[...] = tile_rows(flags, inner[g][:1])
    total = jnp.zeros((256, LANES), jnp.float32)
    for c in range(TILES // CHUNK):
        spot = pl.ds(64 * CHUNK * c, 64 * CHUNK)
        grad_probs = dot_cols(values[spot], grads[g])
        probs, rest = [], []
        for i in range(CHUNK):
            t = c * CHUNK + i
            p = jnp.exp(scores[pl.ds(64 * t, 64)] - lse_rows[pl.ds(t, 1)])
            probs.append(p.astype(jnp.bfloat16))
            rest.append(
                (p * (grad_probs[64 * i : 64 * i + 64] - inner_rows[pl.ds(t, 1)])).astype(jnp.bfloat16)
            )
        probs = jnp.concatenate(probs, axis=0)
        rest = jnp.concatenate(rest, axis=0)
        total = total + dot_rows(keys[spot], rest)
        to_keys = jnp.dot(rest, queries[g], preferred_element_type=jnp.float32)
        to_values = jnp.dot(probs, grads[g], preferred_element_type=jnp.float32)
        left = lax.broadcasted_iota(jnp.int32, (64, 128), 1) < 64
        for i in range(CHUNK):
            t = c * CHUNK + i
            k0 = to_keys[64 * i : 64 * i + 64, :128]
            k1 = to_keys[64 * i : 64 * i + 64, 128:]
            v0 = to_values[64 * i : 64 * i + 64, :128]
            v1 = to_values[64 * i : 64 * i + 64, 128:]
            a = jnp.where(left, pltpu.roll(k0, 64, 1), v0)
            if t < TILES - 1:
                use_a = jnp.broadcast_to(tall[t][:1] > 0.5, (64, 128))
                lo = jnp.where(left, k0, pltpu.roll(v0, 64, 1)) + jnp.where(use_a, a, 0.0)
                hi = jnp.where(use_a, 0.0, jnp.where(left, k1, pltpu.roll(v1, 64, 1)))
                dkv[g, t // 8, (t // 2) % 4, t % 2, :64] = lo.astype(jnp.bfloat16)
                dkv[g, t // 8, (t // 2) % 4, t % 2, 64:] = hi.astype(jnp.bfloat16)
            else:
                spot = (g, me[1], me[2], me[3], pl.ds(0, 64))
                dkv[spot] = (dkv[spot].astype(jnp.float32) + a).astype(jnp.bfloat16)
    dq[g] = fold_lanes(total)


def weight_gather(me, source, whole, sends, recvs, swap_sends, swap_recvs, own_sem):
    def region(k, phase, at, core):
        index = [at[0], at[1], at[2]]
        for i in range(phase):
            index[(k + i) % 3] = slice(None)
        return whole.at[tuple(index) + (core, pl.ds(16 * k, 16))]

    def copy(src, dst, k, phase, s):
        return pltpu.make_async_remote_copy(
            src_ref=src, dst_ref=dst,
            send_sem=sends.at[k, phase, s - 1], recv_sem=recvs.at[k, phase, s - 1],
            device_id=device(*moved(me, (k + phase) % 3, s)), device_id_type=MESH)

    def send(k, phase, s):
        spot = region(k, phase, me, me[3])
        return copy(spot if phase else source.at[pl.ds(16 * k, 16)], spot, k, phase, s)

    def landed(k, phase, s):
        spot = region(k, phase, moved(me, (k + phase) % 3, -s), me[3])
        return copy(spot, spot, k, phase, s)

    def swap(k, s, core):
        spot = region(k, 2, moved(me, (k + 2) % 3, -s), core)
        return pltpu.make_async_remote_copy(
            src_ref=spot, dst_ref=spot,
            send_sem=swap_sends.at[k, s], recv_sem=swap_recvs.at[k, s],
            device_id=device(*sibling(me)), device_id_type=MESH)

    def begin():
        own = pltpu.make_async_copy(source, whole.at[me], own_sem)
        own.start()
        for k in range(3):
            for s in (2, 1, 3):
                send(k, 0, s).start()
        own.wait()

    def forward(phase):
        for k in range(3):
            for s in (1, 3, 2):
                landed(k, phase - 1, s).wait_recv()
            for s in (2, 1, 3):
                send(k, phase, s).start()
            if phase == 2:
                swap(k, 0, me[3]).start()

    def exchange():
        for s in (1, 3, 2):
            for k in range(3):
                landed(k, 2, s).wait_recv()
                swap(k, s, me[3]).start()

    def finish():
        for k in range(3):
            for phase in range(3):
                for s in (1, 2, 3):
                    send(k, phase, s).wait_send()
            for s in range(4):
                swap(k, s, me[3]).wait_send()
                swap(k, s, 1 - me[3]).wait_recv()

    return begin, forward, exchange, finish


WEIGHT_GATHER_SEMS = [
    pltpu.SemaphoreType.DMA((3, 3, 3)),
    pltpu.SemaphoreType.DMA((3, 3, 3)),
    pltpu.SemaphoreType.DMA((3, 4)),
    pltpu.SemaphoreType.DMA((3, 4)),
    pltpu.SemaphoreType.DMA,
]
WHOLE = jax.ShapeDtypeStruct((4, 4, 4, 2, 48, MODEL_WIDTH), jnp.bfloat16)
ALL_PEERS = tuple((a, s) for a in range(3) for s in (1, 2, 3))


def greet_all(me):
    greet([moved(me, a, s) for a, s in ALL_PEERS] + [sibling(me)])


def row_gather(me, own, kv, sends, recvs, swap_sends, swap_recvs, own_sems):
    def region(g, k, phase, at, core):
        index = [at[1], at[2]]
        if phase >= 1:
            index[1 - k] = slice(None)
        return kv.at[(g,) + tuple(index) + (core, pl.ds(64 * k, 64))]

    def axis_of(k, phase):
        return 1 + (1 - k + phase) % 2

    def copy(src, dst, g, k, phase, s):
        return pltpu.make_async_remote_copy(
            src_ref=src, dst_ref=dst,
            send_sem=sends.at[g, k, phase, s - 1], recv_sem=recvs.at[g, k, phase, s - 1],
            device_id=device(*moved(me, axis_of(k, phase), s)), device_id_type=MESH)

    def send(g, k, phase, s):
        spot = region(g, k, phase, me, me[3])
        return copy(spot if phase else own.at[g, pl.ds(64 * k, 64)], spot, g, k, phase, s)

    def landed(g, k, phase, s):
        spot = region(g, k, phase, moved(me, axis_of(k, phase), -s), me[3])
        return copy(spot, spot, g, k, phase, s)

    def swap(g, k, s, core):
        spot = region(g, k, 1, moved(me, axis_of(k, 1), -s), core)
        return pltpu.make_async_remote_copy(
            src_ref=spot, dst_ref=spot,
            send_sem=swap_sends.at[g, k, s], recv_sem=swap_recvs.at[g, k, s],
            device_id=device(*sibling(me)), device_id_type=MESH)

    def keep(g):
        return pltpu.make_async_copy(own.at[g], kv.at[g, me[1], me[2], me[3]], own_sems.at[g])

    def begin(g):
        for s in (2, 1, 3):
            for k in range(2):
                send(g, k, 0, s).start()
        keep(g).start()

    def forward(g):
        keep(g).wait()
        for k in range(2):
            for s in (1, 3, 2):
                landed(g, k, 0, s).wait_recv()
            for s in (2, 1, 3):
                send(g, k, 1, s).start()
            swap(g, k, 0, me[3]).start()

    def arrive(g):
        for s in (1, 3, 2):
            for k in range(2):
                landed(g, k, 1, s).wait_recv()
                swap(g, k, s, me[3]).start()
        for k in range(2):
            for s in range(4):
                swap(g, k, s, 1 - me[3]).wait_recv()

    def finish(g):
        for k in range(2):
            for phase in range(2):
                for s in (1, 2, 3):
                    send(g, k, phase, s).wait_send()
            for s in range(4):
                swap(g, k, s, me[3]).wait_send()

    return begin, forward, arrive, finish


def forward_kernel(
    own, queries, flags, tall, source, out, lse, kv, whole,
    keys, values, scores, rows, *sems
):
    me = place()
    greet_all(me)
    begin, forward, arrive, finish = row_gather(me, own, kv, *sems[:5])
    w_begin, w_forward, w_exchange, w_finish = weight_gather(me, source, whole, *sems[5:])
    for g in range(3):
        begin(g)
    w_begin()
    for g in range(3):
        forward(g)
    w_forward(1)

    def one(g, carry):
        arrive(g)

        @pl.when(g == 1)
        def _():
            w_forward(2)

        attend_group(g, own, kv, queries, flags, tall, out, lse, keys, values, scores, rows)
        return carry

    lax.fori_loop(0, 3, one, 0)
    w_exchange()
    for g in range(3):
        finish(g)
    w_finish()


def attention_forward(own, queries, flags, source):
    vmem = pl.BlockSpec(memory_space=pltpu.VMEM)
    hbm = pl.BlockSpec(memory_space=pl.ANY)
    return pl.pallas_call(
        forward_kernel,
        out_shape=(
            jax.ShapeDtypeStruct((3, 64, LANES), jnp.float32),
            jax.ShapeDtypeStruct((3, 8, LANES), jnp.float32),
            jax.ShapeDtypeStruct((3, 4, 4, 2, 128, 128), jnp.bfloat16),
            WHOLE,
        ),
        in_specs=[vmem, vmem, vmem, vmem, hbm],
        out_specs=(vmem, vmem, vmem, hbm),
        scratch_shapes=[
            pltpu.VMEM((64 * TILES, 256), jnp.bfloat16),
            pltpu.VMEM((64 * TILES, 256), jnp.bfloat16),
            pltpu.VMEM((64 * TILES, LANES), jnp.float32),
            pltpu.VMEM((40, LANES), jnp.float32),
            pltpu.SemaphoreType.DMA((3, 2, 2, 3)),
            pltpu.SemaphoreType.DMA((3, 2, 2, 3)),
            pltpu.SemaphoreType.DMA((3, 2, 4)),
            pltpu.SemaphoreType.DMA((3, 2, 4)),
            pltpu.SemaphoreType.DMA((3,)),
        ] + WEIGHT_GATHER_SEMS,
        compiler_params=pltpu.CompilerParams(
            collective_id=2, has_side_effects=True, vmem_limit_bytes=40 * 2**20
        ),
        name="attention_forward",
    )(own, queries, *flags, source)


def weight_reduce(
    me, planes, out, grads, halves, first, landed_a, sum_a, landed_b, sum_b, landed_c,
    swap_sends, swap_recvs, sends, recvs,
):
    axes = ((2, 1, 0), (0, 2, 1), (1, 0, 2))

    def outer(left, right):
        return dot_rows(left, right).astype(jnp.bfloat16)

    def swap(y):
        return pltpu.make_async_remote_copy(
            src_ref=grads.at[y, :, :, 1 - me[3]], dst_ref=halves.at[y],
            send_sem=swap_sends.at[y], recv_sem=swap_recvs.at[y],
            device_id=device(*sibling(me)), device_id_type=MESH)

    def multiply(y):
        at = 0
        for left, right in planes[y]:
            flat = outer(left[...], right[...])
            count = flat.shape[0] // 48
            cut = flat.reshape(count, 48, MODEL_WIDTH)
            for i in range(count):
                j = at + i
                grads[y, j // 8, (j // 2) % 4, j % 2] = cut[i]
            at += count
        swap(y).start()

    def copy(stage, src, dst, k, s, peer):
        return pltpu.make_async_remote_copy(
            src_ref=src, dst_ref=dst,
            send_sem=sends.at[stage, k, s - 1], recv_sem=recvs.at[stage, k, s - 1],
            device_id=device(*peer), device_id_type=MESH)

    def send(stage, k, s):
        axis = axes[k][stage]
        peer = moved(me, axis, s)
        if stage == 0:
            index = [slice(None)] * 3
            index[axis] = peer[axis]
            return copy(0, first.at[tuple(index) + (pl.ds(16 * k, 16),)], landed_a.at[k, s - 1], k, s, peer)
        if stage == 1:
            index = [slice(None)] * 2
            index[sorted(axes[k][1:]).index(axis)] = peer[axis]
            return copy(1, sum_a.at[(k,) + tuple(index)], landed_b.at[k, s - 1], k, s, peer)
        return copy(2, sum_b.at[k, peer[axis]], landed_c.at[k, s - 1], k, s, peer)

    def halve(y):
        swap(y).wait_recv()
        for x in range(4):
            for z in range(4):
                first[y, x, z] = (
                    grads[y, x, z, me[3]].astype(jnp.float32) + halves[y, x, z].astype(jnp.float32)
                ).astype(jnp.bfloat16)

    def begin():
        for k in range(3):
            for s in (2, 1, 3):
                send(0, k, s).start()

    def second():
        for k in range(3):
            for s in (1, 3, 2):
                send(0, k, s).wait_recv()
            axis = axes[k][0]
            for i in range(4):
                for j in range(4):
                    at = [i, j]
                    at.insert(axis, me[axis])
                    total = first[tuple(at) + (pl.ds(16 * k, 16),)].astype(jnp.float32)
                    for s in range(3):
                        total = total + landed_a[k, s, i, j].astype(jnp.float32)
                    sum_a[k, i, j] = total.astype(jnp.bfloat16)
            for s in (2, 1, 3):
                send(1, k, s).start()

    def third():
        for k in range(3):
            for s in (1, 3, 2):
                send(1, k, s).wait_recv()
            rest = sorted(axes[k][1:])
            for i in range(4):
                at = [i, i]
                at[rest.index(axes[k][1])] = me[axes[k][1]]
                total = sum_a[(k,) + tuple(at)].astype(jnp.float32)
                for s in range(3):
                    total = total + landed_b[k, s, i].astype(jnp.float32)
                sum_b[k, i] = total.astype(jnp.bfloat16)
            for s in (2, 1, 3):
                send(2, k, s).start()

    def finish():
        for k in range(3):
            for s in (1, 3, 2):
                send(2, k, s).wait_recv()
            total = sum_b[k, me[axes[k][2]]].astype(jnp.float32)
            for s in range(3):
                total = total + landed_c[k, s].astype(jnp.float32)
            out[pl.ds(16 * k, 16)] = total
        for y in sorted(planes):
            swap(y).wait_send()
        for stage in range(3):
            for k in range(3):
                for s in (1, 2, 3):
                    send(stage, k, s).wait_send()

    return multiply, halve, begin, second, third, finish


def weight_reduce_scratch():
    bf, w = jnp.bfloat16, MODEL_WIDTH
    return [
        pltpu.VMEM((4, 4, 4, 2, 48, w), bf),
        pltpu.VMEM((4, 4, 4, 48, w), bf),
        pltpu.VMEM((4, 4, 4, 48, w), bf),
        pltpu.VMEM((3, 3, 4, 4, 16, w), bf),
        pltpu.VMEM((3, 4, 4, 16, w), bf),
        pltpu.VMEM((3, 3, 4, 16, w), bf),
        pltpu.VMEM((3, 4, 16, w), bf),
        pltpu.VMEM((3, 3, 16, w), bf),
        pltpu.SemaphoreType.DMA((4,)),
        pltpu.SemaphoreType.DMA((4,)),
        pltpu.SemaphoreType.DMA((3, 3, 3)),
        pltpu.SemaphoreType.DMA((3, 3, 3)),
    ]


def row_reduce(
    me, terms, out, halves, first, landed_a, sum_a, landed_b, swap_sends, swap_recvs, sends, recvs
):
    axes = ((2, 1), (1, 2))

    def swap(g):
        return pltpu.make_async_remote_copy(
            src_ref=terms.at[g, :, :, 1 - me[3]], dst_ref=halves.at[g],
            send_sem=swap_sends.at[g], recv_sem=swap_recvs.at[g],
            device_id=device(*sibling(me)), device_id_type=MESH)

    def send(stage, g, k, s):
        axis = axes[k][stage]
        peer = moved(me, axis, s)
        if stage == 0:
            index = [slice(None)] * 2
            index[axis - 1] = peer[axis]
            src = first.at[(g,) + tuple(index) + (pl.ds(64 * k, 64),)]
            dst = landed_a.at[g, k, s - 1]
        else:
            src = sum_a.at[g, k, peer[axis]]
            dst = landed_b.at[g, k, s - 1]
        return pltpu.make_async_remote_copy(
            src_ref=src, dst_ref=dst,
            send_sem=sends.at[stage, g, k, s - 1], recv_sem=recvs.at[stage, g, k, s - 1],
            device_id=device(*peer), device_id_type=MESH)

    def begin(g):
        swap(g).start()

    def second(g):
        swap(g).wait_recv()
        for x in range(4):
            for z in range(4):
                first[g, x, z] = (
                    terms[g, x, z, me[3]].astype(jnp.float32) + halves[g, x, z].astype(jnp.float32)
                ).astype(jnp.bfloat16)
        for s in (2, 1, 3):
            for k in range(2):
                send(0, g, k, s).start()

    def third(g):
        for k in range(2):
            for s in (1, 3, 2):
                send(0, g, k, s).wait_recv()
            axis = axes[k][0]
            for i in range(4):
                at = [i]
                at.insert(axis - 1, me[axis])
                total = first[(g,) + tuple(at) + (pl.ds(64 * k, 64),)].astype(jnp.float32)
                for s in range(3):
                    total = total + landed_a[g, k, s, i].astype(jnp.float32)
                sum_a[g, k, i] = total.astype(jnp.bfloat16)
            for s in (2, 1, 3):
                send(1, g, k, s).start()

    def finish(g):
        for k in range(2):
            for s in (1, 3, 2):
                send(1, g, k, s).wait_recv()
            total = sum_a[g, k, me[axes[k][1]]].astype(jnp.float32)
            for s in range(3):
                total = total + landed_b[g, k, s].astype(jnp.float32)
            out[g, pl.ds(64 * k, 64)] = total

    def drain(g):
        swap(g).wait_send()
        for stage in range(2):
            for k in range(2):
                for s in (1, 2, 3):
                    send(stage, g, k, s).wait_send()

    return begin, second, third, finish, drain


def row_reduce_scratch():
    bf = jnp.bfloat16
    return [
        pltpu.VMEM((3, 4, 4, 128, 128), bf),
        pltpu.VMEM((3, 4, 4, 128, 128), bf),
        pltpu.VMEM((3, 2, 3, 4, 64, 128), bf),
        pltpu.VMEM((3, 2, 4, 64, 128), bf),
        pltpu.VMEM((3, 2, 3, 64, 128), bf),
        pltpu.SemaphoreType.DMA((3,)),
        pltpu.SemaphoreType.DMA((3,)),
        pltpu.SemaphoreType.DMA((2, 3, 2, 3)),
        pltpu.SemaphoreType.DMA((2, 3, 2, 3)),
    ]


def backward_kernel(shape, *refs):
    count = 1 + max(i for plane in shape.values() for pair in plane for i in pair)
    kv, own, queries, grads, lse, inner, flags, tall = refs[:8]
    arrays = refs[8 : 8 + count]
    dq, sums, owned = refs[8 + count : 11 + count]
    keys, values, scores, lse_rows, inner_rows, dkv = refs[11 + count : 17 + count]
    row_refs = refs[17 + count : 26 + count]
    weight_refs = refs[26 + count :]
    me = place()
    greet_all(me)
    planes = {
        y: [(arrays[i], arrays[j]) for i, j in pairs] for y, pairs in shape.items()
    }
    begin, second, third, finish, drain = row_reduce(me, dkv, sums, *row_refs)
    multiply, halve, w_begin, w_second, w_third, w_finish = weight_reduce(
        me, planes, owned, *weight_refs
    )
    first_sums = weight_refs[2]
    order = sorted(planes, key=lambda y: (y == 0, y))
    for y in order:
        multiply(y)

    def one(g, carry):
        attend_back_group(
            g, me, kv, own, queries, grads, lse, inner, flags, tall, dq, dkv,
            keys, values, scores, lse_rows, inner_rows,
        )
        begin(g)

        @pl.when(g == 0)
        def _():
            for y in order:
                halve(y)
            if 0 not in planes:
                first_sums[0] = jnp.zeros(first_sums.shape[1:], jnp.bfloat16)
            w_begin()

        @pl.when(g == 1)
        def _():
            second(0)

        @pl.when(g == 2)
        def _():
            third(0)
            second(1)
            w_second()

        return carry

    lax.fori_loop(0, 3, one, 0)
    second(2)
    third(1)
    w_third()
    third(2)
    w_finish()
    for g in range(3):
        finish(g)
    for g in range(3):
        drain(g)


def attention_backward(collective_id, shape, kv, own, queries, grads, lse, inner, flags, arrays):
    vmem = pl.BlockSpec(memory_space=pltpu.VMEM)
    return pl.pallas_call(
        functools.partial(backward_kernel, shape),
        out_shape=(
            jax.ShapeDtypeStruct((3, 64, LANES), jnp.float32),
            jax.ShapeDtypeStruct((3, 128, 128), jnp.float32),
            jax.ShapeDtypeStruct((48, MODEL_WIDTH), jnp.float32),
        ),
        in_specs=[vmem] * (8 + len(arrays)),
        out_specs=(vmem,) * 3,
        scratch_shapes=[
            pltpu.VMEM((64 * TILES, 256), jnp.bfloat16),
            pltpu.VMEM((64 * TILES, 256), jnp.bfloat16),
            pltpu.VMEM((64 * TILES, LANES), jnp.float32),
            pltpu.VMEM((40, LANES), jnp.float32),
            pltpu.VMEM((40, LANES), jnp.float32),
            pltpu.VMEM((3, 4, 4, 2, 128, 128), jnp.bfloat16),
        ] + row_reduce_scratch() + weight_reduce_scratch(),
        compiler_params=pltpu.CompilerParams(
            collective_id=collective_id, has_side_effects=True, vmem_limit_bytes=58 * 2**20
        ),
        name="attention_backward",
    )(kv, own, queries, grads, lse, inner, *flags, *arrays)


HALF_ROWS = ((0, 32), (32, 16))


def gather_first_kernel(
    source, extra, whole, extras, stage, sends, recvs, swap_sends, swap_recvs,
    y_sends, y_recvs, extra_sends, extra_recvs, own_sems
):
    me = place()
    greet_all(me)

    def y_copy(src, dst, n, s):
        return pltpu.make_async_remote_copy(
            src_ref=src, dst_ref=dst,
            send_sem=y_sends.at[n, s - 1], recv_sem=y_recvs.at[n, s - 1],
            device_id=device(*moved(me, 0, s)), device_id_type=MESH)

    def rows_along_y(s, y):
        return y_copy(source, stage.at[y], 0, s)

    def extra_region(phase, at, core):
        index = [at[0], at[1], at[2]]
        for axis in (0, 2, 1)[:phase]:
            index[axis] = slice(None)
        return extras.at[tuple(index) + (core,)]

    def extra_copy(phase, s, spot, src, peer):
        return pltpu.make_async_remote_copy(
            src_ref=src, dst_ref=spot,
            send_sem=extra_sends.at[phase, s], recv_sem=extra_recvs.at[phase, s],
            device_id=device(*peer), device_id_type=MESH)

    def extra_send(phase, s):
        spot = extra_region(phase, me, me[3])
        return extra_copy(phase, s, spot, spot if phase else extra, moved(me, (0, 2, 1)[phase], s))

    def extra_landed(phase, s):
        axis = (0, 2, 1)[phase]
        spot = extra_region(phase, moved(me, axis, -s), me[3])
        return extra_copy(phase, s, spot, spot, moved(me, axis, s))

    def extra_swap(core):
        spot = extra_region(3, me, core)
        return extra_copy(3, 0, spot, spot, sibling(me))

    def region(k, phase, at, core):
        index = [at[1], at[2]]
        if phase:
            index[k] = slice(None)
        return whole.at[tuple(index) + (core, pl.ds(*HALF_ROWS[k]))]

    def copy(src, dst, k, phase, s):
        return pltpu.make_async_remote_copy(
            src_ref=src, dst_ref=dst,
            send_sem=sends.at[k, phase, s - 1], recv_sem=recvs.at[k, phase, s - 1],
            device_id=device(*moved(me, 1 + (k + phase) % 2, s)), device_id_type=MESH)

    def send(k, phase, s):
        spot = region(k, phase, me, me[3])
        return copy(spot if phase else stage.at[0, pl.ds(*HALF_ROWS[k])], spot, k, phase, s)

    def landed(k, phase, s):
        spot = region(k, phase, moved(me, 1 + (k + phase) % 2, -s), me[3])
        return copy(spot, spot, k, phase, s)

    def swap(k, s, core):
        spot = region(k, 1, moved(me, 1 + (k + 1) % 2, -s), core)
        return pltpu.make_async_remote_copy(
            src_ref=spot, dst_ref=spot,
            send_sem=swap_sends.at[k, s], recv_sem=swap_recvs.at[k, s],
            device_id=device(*sibling(me)), device_id_type=MESH)

    for s in (2, 1, 3):
        rows_along_y(s, me[0]).start()
        extra_send(0, s).start()
    own = pltpu.make_async_copy(source, stage.at[me[0]], own_sems.at[0])
    own_extra = pltpu.make_async_copy(extra, extras.at[me], own_sems.at[1])
    own.start()
    own_extra.start()
    own.wait()
    own_extra.wait()
    for s in (1, 3, 2):
        rows_along_y(s, (me[0] - s) % RING).wait_recv()
    keep = pltpu.make_async_copy(stage.at[0], whole.at[me[1], me[2], me[3]], own_sems.at[2])
    keep.start()
    for k in range(2):
        for s in (2, 1, 3):
            send(k, 0, s).start()
    for s in (1, 3, 2):
        extra_landed(0, s).wait_recv()
    for s in (2, 1, 3):
        extra_send(1, s).start()
    keep.wait()
    for k in range(2):
        for s in (1, 3, 2):
            landed(k, 0, s).wait_recv()
        for s in (2, 1, 3):
            send(k, 1, s).start()
        swap(k, 0, me[3]).start()
    for s in (1, 3, 2):
        extra_landed(1, s).wait_recv()
    for s in (2, 1, 3):
        extra_send(2, s).start()
    for s in (1, 3, 2):
        for k in (1, 0):
            landed(k, 1, s).wait_recv()
            swap(k, s, me[3]).start()
    for s in (1, 3, 2):
        extra_landed(2, s).wait_recv()
    extra_swap(me[3]).start()
    for s in (1, 2, 3):
        rows_along_y(s, me[0]).wait_send()
        for phase in range(3):
            extra_send(phase, s).wait_send()
    for k in range(2):
        for phase in range(2):
            for s in (1, 2, 3):
                send(k, phase, s).wait_send()
        for s in range(4):
            swap(k, s, me[3]).wait_send()
            swap(k, s, 1 - me[3]).wait_recv()
    extra_swap(me[3]).wait_send()
    extra_swap(1 - me[3]).wait_recv()


def gather_first(source, extra):
    hbm = pl.BlockSpec(memory_space=pl.ANY)
    vmem = pl.BlockSpec(memory_space=pltpu.VMEM)
    return pl.pallas_call(
        gather_first_kernel,
        out_shape=(
            jax.ShapeDtypeStruct((4, 4, 2, 48, MODEL_WIDTH), jnp.bfloat16),
            jax.ShapeDtypeStruct((4, 4, 4, 2, 16, 128), jnp.bfloat16),
        ),
        in_specs=[hbm, hbm],
        out_specs=(hbm, hbm),
        scratch_shapes=[
            pltpu.VMEM((4, 48, MODEL_WIDTH), jnp.bfloat16),
            pltpu.SemaphoreType.DMA((2, 2, 3)),
            pltpu.SemaphoreType.DMA((2, 2, 3)),
            pltpu.SemaphoreType.DMA((2, 4)),
            pltpu.SemaphoreType.DMA((2, 4)),
            pltpu.SemaphoreType.DMA((1, 3)),
            pltpu.SemaphoreType.DMA((1, 3)),
            pltpu.SemaphoreType.DMA((4, 4)),
            pltpu.SemaphoreType.DMA((4, 4)),
            pltpu.SemaphoreType.DMA((3,)),
        ],
        compiler_params=pltpu.CompilerParams(collective_id=1, has_side_effects=True),
        name="gather_first",
    )(source, extra)


def reduce_last_kernel(
    gq, gk, gv, mixed, n1, gb, gains, out, gains_out,
    grads, halves, first, landed_a, sum_a, landed_b, sum_b, landed_y, gain_in, gain_sum,
    swap_sends, swap_recvs, sends, recvs, y_sends, y_recvs, gain_sends, gain_recvs
):
    me = place()
    greet_all(me)

    def gain_copy(stage, s, peer):
        return pltpu.make_async_remote_copy(
            src_ref=gain_sum.at[stage], dst_ref=gain_in.at[stage, s - 1],
            send_sem=gain_sends.at[stage, s - 1], recv_sem=gain_recvs.at[stage, s - 1],
            device_id=device(*peer), device_id_type=MESH)

    def gain_stage(stage, axis):
        total = gain_sum[stage]
        for s in (1,) if stage == 0 else (1, 2, 3):
            gain_copy(stage, s, me if stage else sibling(me)).wait_recv()
            total = total + gain_in[stage, s - 1]
        if axis is None:
            gains_out[...] = total
            return
        gain_sum[stage + 1] = total
        for s in (1, 2, 3):
            gain_copy(stage + 1, s, moved(me, axis, s)).start()

    def swap(x):
        return pltpu.make_async_remote_copy(
            src_ref=grads.at[x, :, 1 - me[3]], dst_ref=halves.at[x],
            send_sem=swap_sends.at[x], recv_sem=swap_recvs.at[x],
            device_id=device(*sibling(me)), device_id_type=MESH)

    def copy(stage, src, dst, k, s):
        return pltpu.make_async_remote_copy(
            src_ref=src, dst_ref=dst,
            send_sem=sends.at[stage, k, s - 1], recv_sem=recvs.at[stage, k, s - 1],
            device_id=device(*moved(me, 1 + (k + 1 + stage) % 2, s)), device_id_type=MESH)

    def send(stage, k, s):
        axis = 1 + (k + 1 + stage) % 2
        to = moved(me, axis, s)[axis]
        rows = pl.ds(*HALF_ROWS[k])
        if stage == 0:
            index = [slice(None)] * 2
            index[axis - 1] = to
            return copy(0, first.at[tuple(index) + (rows,)], landed_a.at[s - 1, :, rows], k, s)
        return copy(1, sum_a.at[to, rows], landed_b.at[s - 1, rows], k, s)

    def y_copy(s):
        return pltpu.make_async_remote_copy(
            src_ref=sum_b, dst_ref=landed_y.at[s - 1],
            send_sem=y_sends.at[s - 1], recv_sem=y_recvs.at[s - 1],
            device_id=device(*moved(me, 0, s)), device_id_type=MESH)

    gain_sum[0] = gains[...]
    gain_copy(0, 1, sibling(me)).start()
    at = 0
    for left, right in ((gq, n1), (gk, n1), (gv, n1), (mixed, gb)):
        flat = dot_rows(left[...], right[...]).astype(jnp.bfloat16)
        amount = flat.shape[0] // 48
        cut = flat.reshape(amount, 48, MODEL_WIDTH)
        for i in range(amount):
            j = at + i
            grads[j // 8, (j // 2) % 4, j % 2] = cut[i]
            if j % 8 == 7:
                swap(j // 8).start()
        at += amount
    gain_stage(0, 2)
    for x in range(4):
        swap(x).wait_recv()
        for z in range(4):
            first[x, z] = (
                grads[x, z, me[3]].astype(jnp.float32) + halves[x, z].astype(jnp.float32)
            ).astype(jnp.bfloat16)
    for k in range(2):
        for s in (2, 1, 3):
            send(0, k, s).start()
    gain_stage(1, 1)
    for k in (1, 0):
        rows = pl.ds(*HALF_ROWS[k])
        for s in (1, 3, 2):
            send(0, k, s).wait_recv()
        axis = 1 + (k + 1) % 2
        for i in range(4):
            spot = [i]
            spot.insert(axis - 1, me[axis])
            total = first[tuple(spot) + (rows,)].astype(jnp.float32)
            for s in range(3):
                total = total + landed_a[s, i, rows].astype(jnp.float32)
            sum_a[i, rows] = total.astype(jnp.bfloat16)
        for s in (2, 1, 3):
            send(1, k, s).start()
    gain_stage(2, 0)
    for k in (1, 0):
        rows = pl.ds(*HALF_ROWS[k])
        for s in (1, 3, 2):
            send(1, k, s).wait_recv()
        total = sum_a[me[1 + k % 2], rows].astype(jnp.float32)
        for s in range(3):
            total = total + landed_b[s, rows].astype(jnp.float32)
        sum_b[rows] = total.astype(jnp.bfloat16)
    for s in (2, 1, 3):
        y_copy(s).start()
    gain_stage(3, None)
    total = sum_b[...].astype(jnp.float32)
    for s in (1, 3, 2):
        y_copy(s).wait_recv()
        total = total + landed_y[s - 1].astype(jnp.float32)
    out[...] = total
    for x in range(4):
        swap(x).wait_send()
    for stage in range(2):
        for k in range(2):
            for s in (1, 2, 3):
                send(stage, k, s).wait_send()
    gain_copy(0, 1, sibling(me)).wait_send()
    for s in (1, 2, 3):
        y_copy(s).wait_send()
        for stage, axis in ((1, 2), (2, 1), (3, 0)):
            gain_copy(stage, s, moved(me, axis, s)).wait_send()


def reduce_last(arrays, gains):
    bf, w = jnp.bfloat16, MODEL_WIDTH
    vmem = pl.BlockSpec(memory_space=pltpu.VMEM)
    rows = gains.shape[0]
    return pl.pallas_call(
        reduce_last_kernel,
        out_shape=(
            jax.ShapeDtypeStruct((48, w), jnp.float32),
            jax.ShapeDtypeStruct(gains.shape, jnp.float32),
        ),
        in_specs=[vmem] * 7,
        out_specs=(vmem, vmem),
        scratch_shapes=[
            pltpu.VMEM((4, 4, 2, 48, w), bf),
            pltpu.VMEM((4, 4, 48, w), bf),
            pltpu.VMEM((4, 4, 48, w), bf),
            pltpu.VMEM((3, 4, 48, w), bf),
            pltpu.VMEM((4, 48, w), bf),
            pltpu.VMEM((3, 48, w), bf),
            pltpu.VMEM((48, w), bf),
            pltpu.VMEM((3, 48, w), bf),
            pltpu.VMEM((4, 3, rows, 128), jnp.float32),
            pltpu.VMEM((4, rows, 128), jnp.float32),
            pltpu.SemaphoreType.DMA((4,)),
            pltpu.SemaphoreType.DMA((4,)),
            pltpu.SemaphoreType.DMA((2, 2, 3)),
            pltpu.SemaphoreType.DMA((2, 2, 3)),
            pltpu.SemaphoreType.DMA((3,)),
            pltpu.SemaphoreType.DMA((3,)),
            pltpu.SemaphoreType.DMA((4, 3)),
            pltpu.SemaphoreType.DMA((4, 3)),
        ],
        compiler_params=pltpu.CompilerParams(
            collective_id=5, has_side_effects=True, vmem_limit_bytes=32 * 2**20
        ),
        name="reduce_last",
    )(*arrays, gains)


def rotation_parts(places, heads):
    feature_width = heads * HEAD_SIZE
    half_size = HEAD_SIZE // 2
    feature_index = jnp.arange(feature_width)
    within = feature_index % HEAD_SIZE
    pair_index = within % half_size
    frequency = 1.0 / THETA ** ((2 * pair_index).astype(jnp.float32) / HEAD_SIZE)
    phases = places.astype(jnp.float32)[:, None] * frequency[None, :]
    head_of = feature_index // HEAD_SIZE
    same_head = head_of[:, None] == head_of[None, :]
    lower_target = within[None, :] < half_size
    from_upper = (within[:, None] == within[None, :] + half_size) & lower_target
    from_lower = (within[:, None] + half_size == within[None, :]) & jnp.logical_not(lower_target)
    swapper = jnp.where(
        same_head & from_upper, -1.0, jnp.where(same_head & from_lower, 1.0, 0.0)
    ).astype(jnp.float32)
    return (jnp.cos(phases), jnp.sin(phases), swapper)


def apply_rotation(values, parts):
    cosine_wide, sine_wide, swapper = parts
    swapped = jnp.dot(values, swapper, precision=HIGHEST)
    return values * cosine_wide + swapped * sine_wide


def inverse_rotation(values, parts):
    cosine_wide, sine_wide, swapper = parts
    swapped = jnp.dot(values, swapper, precision=HIGHEST)
    return values * cosine_wide - swapped * sine_wide


def rms_inverse(values):
    return lax.rsqrt(jnp.mean(values * values, -1, keepdims=True) + EPSILON)


def norm_backward(grad_normed, values, inverse, gain):
    unit_rows = values * inverse
    grad_gain = jnp.sum(grad_normed * unit_rows, 0)
    scaled = grad_normed * gain.astype(jnp.float32)
    grad_values = inverse * (scaled - unit_rows * jnp.mean(scaled * unit_rows, -1, keepdims=True))
    return (grad_values, grad_gain)


def by_group(rows):
    return rows.reshape(128, QUERY_HEADS, HEAD_SIZE).transpose(1, 0, 2).reshape(3, LANES, HEAD_SIZE)


def spread(rows):
    parts = rows.reshape(128, QUERY_HEADS, HEAD_SIZE).transpose(1, 0, 2)
    lo, hi = parts[:, :64], parts[:, 64:]
    zero = jnp.zeros_like(lo)
    top = jnp.concatenate([zero, lo, hi, zero], -1)
    low = jnp.concatenate([hi, zero, zero, zero], -1)
    return jnp.concatenate([top, low], 1).reshape(3, LANES, 256)


def by_token(turned):
    return turned.reshape(3, HEAD_SIZE, 3, 128).transpose(3, 0, 2, 1).reshape(128, MODEL_WIDTH)


def paired(keys, values):
    both = jnp.stack([keys.reshape(128, 3, 64), values.reshape(128, 3, 64)], 2)
    return both.reshape(128, 3, 128).transpose(1, 0, 2)


def layer_forward(hidden, first, gains, flags, source, query_parts, key_parts):
    query_t, key_t, value_t, w_out = jnp.split(first, (576, 768, 960), axis=0)
    inverse_one = rms_inverse(hidden)
    normed_one = (hidden * inverse_one * gains[:MODEL_WIDTH].astype(jnp.float32)).astype(jnp.bfloat16)
    query_rows = apply_rotation(dot_cols(normed_one, query_t), query_parts).astype(jnp.bfloat16)
    key_rows = apply_rotation(dot_cols(normed_one, key_t), key_parts).astype(jnp.bfloat16)
    value_rows = dot_cols(normed_one, value_t).astype(jnp.bfloat16)
    own = paired(key_rows, value_rows)
    queries = spread(query_rows * jnp.bfloat16(HEAD_SIZE ** (-0.5)))
    turned, lse, kv, whole = attention_forward(own, queries, flags, source)
    whole = whole.reshape(4, 1536, MODEL_WIDTH)
    gate_t, up_t, w_down = whole[1], whole[2], whole[3]
    mixed = by_token(turned).astype(jnp.bfloat16)
    middle = hidden + jnp.dot(mixed, w_out, preferred_element_type=jnp.float32)
    inverse_two = rms_inverse(middle)
    normed_two = (middle * inverse_two * gains[MODEL_WIDTH:].astype(jnp.float32)).astype(jnp.bfloat16)
    gate_values = dot_cols(normed_two, gate_t)
    up_values = dot_cols(normed_two, up_t)
    product = (jax.nn.silu(gate_values) * up_values).astype(jnp.bfloat16)
    result = middle + jnp.dot(product, w_down, preferred_element_type=jnp.float32)
    kept = (
        hidden, inverse_one, normed_one, queries, own, kv, turned, lse, mixed,
        middle, inverse_two, normed_two, gate_values, up_values, product,
        (query_t, key_t, value_t, w_out, gate_t, up_t, w_down),
    )
    return result, kept, whole[0]


def layer_backward(grad_result, kept, gains, flags, more, query_parts, key_parts):
    (
        hidden, inverse_one, normed_one, queries, own, kv, turned, lse, mixed,
        middle, inverse_two, normed_two, gate_values, up_values, product,
        (query_t, key_t, value_t, w_out, gate_t, up_t, w_down),
    ) = kept
    grad_down = grad_result.astype(jnp.bfloat16)
    grad_product = dot_cols(grad_down, w_down)
    sigmoid_values = jax.nn.sigmoid(gate_values)
    grad_gate = (
        grad_product * up_values * (sigmoid_values * (1.0 + gate_values * (1.0 - sigmoid_values)))
    ).astype(jnp.bfloat16)
    grad_up = (grad_product * (gate_values * sigmoid_values)).astype(jnp.bfloat16)
    grad_normed_two = jnp.dot(grad_gate, gate_t, preferred_element_type=jnp.float32) + jnp.dot(
        grad_up, up_t, preferred_element_type=jnp.float32
    )
    grad_middle, grad_gain_two = norm_backward(
        grad_normed_two, middle, inverse_two, gains[MODEL_WIDTH:]
    )
    grad_middle = grad_middle + grad_result
    grad_branch = grad_middle.astype(jnp.bfloat16)
    grad_mixed = dot_cols(grad_branch, w_out).astype(jnp.bfloat16)
    inner = jnp.sum(
        turned * by_group(grad_mixed).astype(jnp.float32).transpose(0, 2, 1), 1, keepdims=True
    )
    inner = jnp.broadcast_to(inner, (3, 8, LANES))
    arrays = (grad_gate, grad_up, product, normed_two, grad_down)
    shape = {1: ((0, 3),), 2: ((1, 3),), 3: ((2, 4),)}
    if more is not None:
        arrays = arrays + more
        shape[0] = ((5, 9), (6, 9), (7, 9), (8, 10))
    dq, sums, owned = attention_backward(
        3 if more is None else 4, shape,
        kv, own, queries, spread(grad_mixed), lse, inner, flags, arrays,
    )
    sums = sums.transpose(1, 0, 2).reshape(128, 3, 2, 64)
    key_sums = sums[:, :, 0].reshape(128, 192)
    value_sums = sums[:, :, 1].reshape(128, 192)
    grad_query = by_token(dq) * HEAD_SIZE ** (-0.5)
    grad_query = inverse_rotation(grad_query, query_parts).astype(jnp.bfloat16)
    key_gradient = inverse_rotation(key_sums, key_parts).astype(jnp.bfloat16)
    value_gradient = value_sums.astype(jnp.bfloat16)
    grad_normed_one = (
        jnp.dot(grad_query, query_t, preferred_element_type=jnp.float32)
        + jnp.dot(key_gradient, key_t, preferred_element_type=jnp.float32)
        + jnp.dot(value_gradient, value_t, preferred_element_type=jnp.float32)
    )
    grad_hidden, grad_gain_one = norm_backward(
        grad_normed_one, hidden, inverse_one, gains[:MODEL_WIDTH]
    )
    grad_hidden = grad_hidden + grad_middle
    gain_terms = jnp.concatenate([grad_gain_one, grad_gain_two, jnp.zeros(896, jnp.float32)])
    left = (grad_query, key_gradient, value_gradient, mixed, normed_one, grad_branch)
    return grad_hidden, owned, left, gain_terms.reshape(16, 128)


def on_device(hidden_in, positions, params, gains, cotangent):
    places = positions[0]
    block = places[0] // 64
    turn = block >= 32
    block = jnp.minimum(block, 63 - block)

    def lo_first(rows):
        return jnp.where(turn, jnp.concatenate([rows[64:], rows[:64]], 0), rows)

    places = lo_first(places)
    extra = jnp.concatenate(
        [jnp.pad(gains, ((0, 0), (0, 119))), jnp.full((14, 128), block, jnp.bfloat16)], 0
    )
    at_front = lax.axis_index("fsdp") == 0
    sources = (jnp.where(at_front, params[1], params[0]), params[1])
    first, extras = gather_first(params[0], extra)
    first = first.reshape(1536, MODEL_WIDTH)
    extras = extras.reshape(128, 16, 128)
    gain_rows = [extras[:, layer, :9].reshape(-1) for layer in range(LAYERS)]
    blocks = lax.dynamic_slice(
        extras[:, 2, 0], (lax.axis_index("fsdp") * 32,), (32,)
    ).astype(jnp.int32)
    flags = jnp.concatenate([blocks < block, jnp.full((8,), True)]).astype(jnp.float32)
    flags = (
        jnp.broadcast_to(flags[:, None], (40, LANES)),
        jnp.broadcast_to(flags[:, None, None], (40, 8, 128)),
    )
    query_parts = rotation_parts(places, QUERY_HEADS)
    key_parts = rotation_parts(places, KEY_VALUE_HEADS)
    hidden = lo_first(hidden_in[0]).astype(jnp.float32)
    kept = []
    for layer in range(LAYERS):
        hidden, state, first = layer_forward(
            hidden, first, gain_rows[layer], flags, sources[layer], query_parts, key_parts
        )
        kept.append(state)
    output_rows = lo_first(hidden.astype(jnp.bfloat16))
    grad_hidden = lo_first(cotangent[0]).astype(jnp.float32)
    owned = [None] * LAYERS
    gain_terms = [None] * LAYERS
    left = None
    for layer in reversed(range(LAYERS)):
        grad_hidden, owned[layer], left, gain_terms[layer] = layer_backward(
            grad_hidden, kept[layer], gain_rows[layer], flags, left, query_parts, key_parts
        )
    last, gain_sums = reduce_last(left, jnp.concatenate(gain_terms, 0))
    owned = [jnp.where(at_front, last, owned[0]), jnp.where(at_front, owned[0], owned[1])]
    index = lax.axis_index("fsdp") * 32 + lax.axis_index("ctx")
    owned_gains = lax.dynamic_slice(gain_sums.reshape(LAYERS, 2048), (0, index * 9), (LAYERS, 9))
    return (
        output_rows[None],
        lo_first(grad_hidden)[None],
        jnp.stack(owned),
        owned_gains,
    )


def solution(mesh):
    return jax.shard_map(
        on_device,
        mesh=mesh,
        in_specs=(
            P("fsdp", "ctx", None),
            P("fsdp", "ctx"),
            P(None, ("fsdp", "ctx"), None),
            P(None, ("fsdp", "ctx")),
            P("fsdp", "ctx", None),
        ),
        out_specs=(
            P("fsdp", "ctx", None),
            P("fsdp", "ctx", None),
            P(None, ("fsdp", "ctx"), None),
            P(None, ("fsdp", "ctx")),
        ),
        check_vma=False,
    )
```

time: 878 us -> 359 us (0.41)
  waiting for transfers between devices: 475 us -> 0 us
  Pallas kernels: 0 us -> 244 us
  matrix products: 166 us -> 46.2 us
  blocking collectives: 79.4 us -> 0 us
  other arithmetic: 52.5 us -> 11.3 us
  local copies, waits for them, and re-layouts: 74.9 us -> 45.5 us
  between operations: 17.5 us -> 5.41 us
    reduce_scatter x4 -> x0, waiting for transfers between devices: 244 us -> none  [the longest x2 147 us: sum_packed(): lax.psum_scatter(lines, axis, tiled=True).reshape(-1)]
    pallas_call x0 -> x6, Pallas kernels: none -> 244 us  [the longest x2 103 us: attention_backward(): pl.pallas_call(functools.partial(backward_kernel, shape), out_shape=(jax....]
    all_gather x4 -> x0, waiting for transfers between devices: 119 us -> none  [the longest x2 62.4 us: side_by_side(): lax.all_gather(both, axis, axis=dim, tiled=True)]
    unnamed x12 -> x0, waiting for transfers between devices: 106 us -> none
    dot_general x64 -> x14, matrix products: 125 us -> 20.5 us  [dot_cols(): lax.dot_general(left, right, (((1,), (1,)), ((), ())), preferred_element_...]
    unnamed x2 -> x0, blocking collectives: 79.4 us -> none
    convert_element_type x11 -> x12, other arithmetic: 35.1 us -> 3.6 us  [the longest x2 1.63 us: layer_backward(): grad_branch = grad_middle.astype(jnp.bfloat16)]
    concatenate x2 -> x7, local copies, waits for them, and re-layouts: 22.3 us -> 3.95 us  [the longest x4 3.72 us: spread(): return jnp.concatenate([top, low], 1).reshape(3, LANES, 256)]
  transfers between devices with their start and end apart: 11 -> 0, of which waited for: 11 -> 0; matrix products, arithmetic and copies ran while one was open for 16% -> 0% of each run, Pallas kernels for 0% -> 0%
where the time goes in v1:
time: 359 us; the launch traced here: 352 us
  Pallas kernels  244 us (68%)
  matrix products  46.2 us (13%)
  local copies, waits for them, and re-layouts  45.5 us (13%)
  other arithmetic  11.3 us (3%)
  between operations  5.41 us (2%)
    pallas_call x2, Pallas kernels, attention_backward(): pl.pallas_call(functools.partial(backward_kernel, shape), out_shape=(jax....  103 us
    pallas_call x2, Pallas kernels, attention_forward(): pl.pallas_call(forward_kernel, out_shape=(jax.ShapeDtypeStruct((3, 64, LA...  86.2 us
    pallas_call x1, Pallas kernels, gather_first(): pl.pallas_call(gather_first_kernel, out_shape=(jax.ShapeDtypeStruct((4, 4...  28.6 us
    pallas_call x1, Pallas kernels, reduce_last(): pl.pallas_call(reduce_last_kernel, out_shape=(jax.ShapeDtypeStruct((48, w...  25.9 us
    dot_general x14, matrix products, dot_cols(): lax.dot_general(left, right, (((1,), (1,)), ((), ())), preferred_element_...  20.5 us
    unnamed x241, local copies, waits for them, and re-layouts  16.2 us
    dot_general x4, matrix products, inverse_rotation(): swapped = jnp.dot(values, swapper, precision=HIGHEST)  8.75 us
    dot_general x4, matrix products, apply_rotation(): swapped = jnp.dot(values, swapper, precision=HIGHEST)  7.85 us

profile of v1, /device:TPU:1, one launch (start us, length us, event | category | flops | bytes accessed | tf_op | source)
XLA Modules:
  0.0 351.9 jit_solution(5225293693547727159)
XLA Ops:
  3.2 1.3 fusion.116.extra
  4.5 1.5 slice_bitcast_fusion.2
  6.0 28.6 %gather_first.1 = (bf16[4,4,2,48,576]{4,3,2,1,0:T(8,128)(2,1)}, bf16[4,4,4,2,16,128]{5,4,3,2,1,0:T(8,128)(2,1)}) custom-call(bf16[48,576]{1,0:T(8,128)(2,1)} %get-tuple-element.105.source, bf16[16,128]{1,0:T(8,128)(2,1)} %fusion.116.extra), custom_call_target="tpu_custom_call" | custom-call | tf_op jit(solution)/shard_map/gather_first/pallas_call | solution.py:859
  34.6 1.2 fusion.168
  38.4 1.5 fusion.55
  40.3 3.1 fusion.21
  44.8 1.4 fusion.91
  48.5 1.2 convolution_convert_fusion.3
  51.3 42.4 %attention_forward.2 = (f32[3,64,384]{2,1,0:T(8,128)S(1)}, f32[3,8,384]{2,1,0:T(8,128)S(1)}, bf16[3,4,4,2,128,128]{5,4,3,2,1,0:T(8,128)(2,1)S(1)}, bf16[4,4,4,2,48,576]{5,4,3,2,1,0:T(8,128)(2,1)S(1)}) custom-call(bf16[3,128,128]{2,1,0:T(8,128)(2,1)S(1)} %bitcast.171, bf16[3,384,256]{2,1,0:T(8,128)(2,1)S(1)} %bitcast.167, ...), custom_call_target="tpu_custom_call" | custom-call | tf_op jit(solution)/shard_map/attention_forward/pallas_call | solution.py:401
  93.8 2.6 fusion.167
  97.4 2.1 multiply_reduce_fusion.8
  101.4 1.8 multiply_convert_fusion.5
  104.8 1.5 fusion.49
  106.6 3.0 fusion.22
  110.5 1.4 fusion.86
  113.0 1.2 convolution_convert_fusion.2
  114.4 43.8 %attention_forward.3 = (f32[3,64,384]{2,1,0:T(8,128)S(1)}, f32[3,8,384]{2,1,0:T(8,128)S(1)}, bf16[3,4,4,2,128,128]{5,4,3,2,1,0:T(8,128)(2,1)S(1)}, bf16[4,4,4,2,48,576]{5,4,3,2,1,0:T(8,128)(2,1)S(1)}) custom-call(bf16[3,128,128]{2,1,0:T(8,128)(2,1)S(1)} %bitcast.173, bf16[3,384,256]{2,1,0:T(8,128)(2,1)S(1)} %bitcast.169, ...), custom_call_target="tpu_custom_call" | custom-call | tf_op jit(solution)/shard_map/attention_forward/pallas_call | solution.py:401
  158.2 3.0 fusion.166
  162.6 1.5 multiply_reduce_fusion.6
  166.3 1.7 fusion.177
  167.9 1.7 fusion.176
  170.7 3.7 %multiply_convert_fusion.2 = (bf16[128,1536]{1,0:T(8,128)(2,1)S(1)}, bf16[128,1536]{1,0:T(8,128)(2,1)S(1)}, bf16[128,1536]{1,0:T(8,128)(2,1)}) fusion(f32[128,1536]{1,0:T(8,128)} %fusion.176, f32[128,1536]{1,0:T(8,128)} %fusion.177, bf16[1536,576]{1,0:T(8,128)(2,1)} %bitcast.191, bf16[1,128,576]{2,1,0:T(8,128)(2,1)S(1)} %copy.167, ...), kind=kOutput, calls=%fused_computation.63 | convolution fusion | flops 229810176 | bytes 4816897 | tf_op jit(solution)/shard_map/dot_general | solution.py:102
  176.5 1.5 convolution_convert_fusion.1
  180.5 50.3 %attention_backward.2 = (f32[3,64,384]{2,1,0:T(8,128)}, f32[3,128,128]{2,1,0:T(8,128)}, f32[48,576]{1,0:T(8,128)}) custom-call(bf16[3,4,4,2,128,128]{5,4,3,2,1,0:T(8,128)(2,1)} %copy-done.4, bf16[3,128,128]{2,1,0:T(8,128)(2,1)} %bitcast.174, bf16[3,384,256]{2,1,0:T(8,128)(2,1)} %bitcast.170, bf16[3,384,256]{2,1,0:T(8,128)(2,1)} %bitcast.204, ...), custom_call_target="tpu_custom_call" | custom-call | tf_op jit(solution)/shard_map/attention_backward/pallas_call | solution.py:708
  233.7 3.0 fusion.18.refs_13_
  246.4 1.2 reshape.406
  250.4 2.2 copy.187
  254.2 52.5 %attention_backward.3 = (f32[3,64,384]{2,1,0:T(8,128)}, f32[3,128,128]{2,1,0:T(8,128)}, f32[48,576]{1,0:T(8,128)}) custom-call(bf16[3,4,4,2,128,128]{5,4,3,2,1,0:T(8,128)(2,1)} %copy-done.3, bf16[3,128,128]{2,1,0:T(8,128)(2,1)} %bitcast.172, bf16[3,384,256]{2,1,0:T(8,128)(2,1)} %bitcast.168, bf16[3,384,256]{2,1,0:T(8,128)(2,1)} %bitcast.203, ...), custom_call_target="tpu_custom_call" | custom-call | tf_op jit(solution)/shard_map/attention_backward/pallas_call | solution.py:708
  312.6 4.0 %fusion.17.gq = bf16[128,576]{1,0:T(8,128)(2,1)S(1)} fusion(f32[128,576]{0,1:T(8,128)} %bitcast.218, f32[128,576]{1,0:T(8,128)S(1)} %copy.193, f32[128]{0:T(128)S(1)} %copy-done.100, f32[576]{0:T(1024)S(1)} %copy-done.81, s32[576]{0:T(1024)S(1)} %copy-done.79, s32[576]{0:T(1024)S(1)} %copy-done.75, s32[576]{0:T(1024)S(1)} %copy-done.77, ...), kind=kOutput, calls=%fused_computation.39 | convolution fusion | flops 512962560 | bytes 748160 | tf_op jit(solution)/shard_map/dot_general | solution.py:1072
  319.0 25.9 %reduce_last.1 = (f32[48,576]{1,0:T(8,128)S(1)}, f32[32,128]{1,0:T(8,128)S(1)}) custom-call(bf16[128,576]{1,0:T(8,128)(2,1)S(1)} %fusion.17.gq, bf16[128,192]{1,0:T(8,128)(2,1)S(1)} %fusion.30.gk, bf16[128,192]{1,0:T(8,128)(2,1)S(1)} %copy.201.gv, bf16[128,576]{1,0:T(8,128)(2,1)S(1)} %copy.202.mixed, bf16[128,576]{1,0:T(8,128)(2,1)S(1)} %fusion.73.n1, ...), custom_call_target="tpu_custom_call" | custom-call | tf_op jit(solution)/shard_map/reduce_last/pallas_call | solution.py:1010
  346.3 1.4 fusion.77
  348.5 1.8 copy.204
  (369 shorter events, 51.6 us)
Async XLA Ops:
  40.2 6.2 %copy-start.97 = (f32[128]{0:T(128)}, f32[128]{0:T(128)S(1)}, u32[]{:S(2)}) copy-start(f32[128]{0:T(128)S(1)} %fusion.136) | copy-start | bytes 1540
  40.2 66.4 %copy-start.74 = (s32[576]{0:T(1024)}, s32[576]{0:T(1024)S(1)}, u32[]{:S(2)}) copy-start(s32[576]{0:T(1024)S(1)} %get-tuple-element.128) | copy-start | bytes 6916
  40.2 66.4 %copy-start.76 = (s32[576]{0:T(1024)}, s32[576]{0:T(1024)S(1)}, u32[]{:S(2)}) copy-start(s32[576]{0:T(1024)S(1)} %get-tuple-element.129) | copy-start | bytes 6916
  40.2 66.3 %copy-start.78 = (s32[576]{0:T(1024)}, s32[576]{0:T(1024)S(1)}, u32[]{:S(2)}) copy-start(s32[576]{0:T(1024)S(1)} %broadcast_add_fusion) | copy-start | bytes 6916
  40.2 66.3 %copy-start.80 = (f32[576]{0:T(1024)}, f32[576]{0:T(1024)S(1)}, u32[]{:S(2)}) copy-start(f32[576]{0:T(1024)S(1)} %fusion.122) | copy-start | bytes 6916
  44.8 6.5 %copy-start = (bf16[9,128,256]{2,1,0:T(8,128)(2,1)}, bf16[9,128,256]{2,1,0:T(8,128)(2,1)S(1)}, u32[]{:S(2)}) copy-start(bf16[9,128,256]{2,1,0:T(8,128)(2,1)S(1)} %copy.147) | copy-start | bytes 1769476
  44.8 6.5 %copy-start.52 = (bf16[2,48,576]{2,1,0:T(8,128)(2,1)S(1)}, bf16[2,48,576]{2,1,0:T(8,128)(2,1)}, u32[]{:S(2)}) copy-start(bf16[2,48,576]{2,1,0:T(8,128)(2,1)} %param.7) | copy-start | bytes 331780
  49.9 46.6 %copy-start.6 = (bf16[128,3,128]{2,0,1:T(8,128)(2,1)}, bf16[128,3,128]{2,0,1:T(8,128)(2,1)S(1)}, u32[]{:S(2)}) copy-start(bf16[128,3,128]{2,0,1:T(8,128)(2,1)S(1)} %copy.142) | copy-start | bytes 294916
  51.2 63.2 %copy-start.2 = (f32[40,8,128]{2,1,0:T(8,128)}, f32[40,8,128]{2,1,0:T(8,128)S(1)}, u32[]{:S(2)}) copy-start(f32[40,8,128]{2,1,0:T(8,128)S(1)} %broadcast_in_dim.43.tall.refs_7_) | copy-start | bytes 491524
  51.3 63.1 %copy-start.5 = (f32[40,384]{1,0:T(8,128)}, f32[40,384]{1,0:T(8,128)S(1)}, u32[]{:S(2)}) copy-start(f32[40,384]{1,0:T(8,128)S(1)} %broadcast_in_dim.42.flags.refs_6_) | copy-start | bytes 184324
  103.9 5.7 %copy-start.72 = (f32[128]{0:T(128)}, f32[128]{0:T(128)S(1)}, u32[]{:S(2)}) copy-start(f32[128]{0:T(128)S(1)} %add_rsqrt_fusion.1) | copy-start | bytes 1540
  104.7 4.9 %copy-start.62 = (f32[576]{0:T(1024)}, f32[576]{0:T(1024)S(1)}, u32[]{:S(2)}) copy-start(f32[576]{0:T(1024)S(1)} %reshape.403) | copy-start | bytes 6916
  104.8 8.2 %copy-start.24 = (bf16[128,576]{1,0:T(8,128)(2,1)}, bf16[128,576]{1,0:T(8,128)(2,1)S(1)}, u32[]{:S(2)}) copy-start(bf16[128,576]{1,0:T(8,128)(2,1)S(1)} %multiply_convert_fusion.7.refs_17_) | copy-start | bytes 442372
  110.5 47.7 %copy-start.1 = (bf16[9,128,256]{2,1,0:T(8,128)(2,1)}, bf16[9,128,256]{2,1,0:T(8,128)(2,1)S(1)}, u32[]{:S(2)}) copy-start(bf16[9,128,256]{2,1,0:T(8,128)(2,1)S(1)} %copy.162) | copy-start | bytes 1769476
  114.4 46.9 %copy-start.7 = (bf16[128,3,128]{2,0,1:T(8,128)(2,1)}, bf16[128,3,128]{2,0,1:T(8,128)(2,1)S(1)}, u32[]{:S(2)}) copy-start(bf16[128,3,128]{2,0,1:T(8,128)(2,1)S(1)} %copy.158) | copy-start | bytes 294916
  180.4 51.6 %copy-start.91 = (s32[192]{0:T(256)S(1)}, s32[192]{0:T(256)}, u32[]{:S(2)}) copy-start(s32[192]{0:T(256)} %copy-done.89) | copy-start | bytes 2308
  180.4 51.6 %copy-start.95 = (s32[192]{0:T(256)S(1)}, s32[192]{0:T(256)}, u32[]{:S(2)}) copy-start(s32[192]{0:T(256)} %copy-done.93) | copy-start | bytes 2308
  180.4 51.6 %copy-start.99 = (f32[128]{0:T(128)S(1)}, f32[128]{0:T(128)}, u32[]{:S(2)}) copy-start(f32[128]{0:T(128)} %copy-done.97) | copy-start | bytes 1540
  180.4 51.6 %copy-start.103 = (s32[192]{0:T(256)S(1)}, s32[192]{0:T(256)}, u32[]{:S(2)}) copy-start(s32[192]{0:T(256)} %copy-done.101) | copy-start | bytes 2308
  180.4 51.6 %copy-start.107 = (f32[192]{0:T(256)S(1)}, f32[192]{0:T(256)}, u32[]{:S(2)}) copy-start(f32[192]{0:T(256)} %copy-done.105) | copy-start | bytes 2308
  180.5 51.6 %copy-start.111 = (pred[192]{0:T(512)(128)(4,1)S(1)}, pred[192]{0:T(512)(128)(4,1)}, u32[]{:S(2)}) copy-start(pred[192]{0:T(512)(128)(4,1)} %copy-done.109) | copy-start | bytes 580
  180.5 51.6 %copy-start.115 = (pred[192]{0:T(512)(128)(4,1)S(1)}, pred[192]{0:T(512)(128)(4,1)}, u32[]{:S(2)}) copy-start(pred[192]{0:T(512)(128)(4,1)} %copy-done.113) | copy-start | bytes 580
  247.6 5.7 %copy-start.46 = (bf16[128,3,3,64]{0,3,2,1:T(8,128)(2,1)S(1)}, bf16[128,3,3,64]{0,3,2,1:T(8,128)(2,1)}, u32[]{:S(2)}) copy-start(bf16[128,3,3,64]{0,3,2,1:T(8,128)(2,1)} %copy-done.45) | copy-start | bytes 442372
  254.1 53.8 %copy-start.92 = (s32[192]{0:T(256)S(1)}, s32[192]{0:T(256)}, u32[]{:S(2)}) copy-start(s32[192]{0:T(256)} %copy-done.89) | copy-start | bytes 2308
  254.1 53.8 %copy-start.96 = (s32[192]{0:T(256)S(1)}, s32[192]{0:T(256)}, u32[]{:S(2)}) copy-start(s32[192]{0:T(256)} %copy-done.93) | copy-start | bytes 2308
  254.2 53.8 %copy-start.100 = (f32[128]{0:T(128)S(1)}, f32[128]{0:T(128)}, u32[]{:S(2)}) copy-start(f32[128]{0:T(128)} %copy-done.97) | copy-start | bytes 1540
  254.2 53.9 %copy-start.104 = (s32[192]{0:T(256)S(1)}, s32[192]{0:T(256)}, u32[]{:S(2)}) copy-start(s32[192]{0:T(256)} %copy-done.101) | copy-start | bytes 2308
  254.2 53.9 %copy-start.108 = (f32[192]{0:T(256)S(1)}, f32[192]{0:T(256)}, u32[]{:S(2)}) copy-start(f32[192]{0:T(256)} %copy-done.105) | copy-start | bytes 2308
  254.2 53.9 %copy-start.112 = (pred[192]{0:T(512)(128)(4,1)S(1)}, pred[192]{0:T(512)(128)(4,1)}, u32[]{:S(2)}) copy-start(pred[192]{0:T(512)(128)(4,1)} %copy-done.109) | copy-start | bytes 580
  254.2 53.9 %copy-start.116 = (pred[192]{0:T(512)(128)(4,1)S(1)}, pred[192]{0:T(512)(128)(4,1)}, u32[]{:S(2)}) copy-start(pred[192]{0:T(512)(128)(4,1)} %copy-done.113) | copy-start | bytes 580
  317.2 27.7 %copy-start.57 = (f32[48,576]{1,0:T(8,128)S(1)}, f32[48,576]{1,0:T(8,128)}, u32[]{:S(2)}) copy-start(f32[48,576]{1,0:T(8,128)} %get-tuple-element.38) | copy-start | bytes 331780
  317.2 27.7 %copy-start.58 = (f32[48,576]{1,0:T(8,128)S(1)}, f32[48,576]{1,0:T(8,128)}, u32[]{:S(2)}) copy-start(f32[48,576]{1,0:T(8,128)} %get-tuple-element.37) | copy-start | bytes 331780
  (86 other events, 163.1 us)

commit v2 on v1

--- a/solution.py
+++ b/solution.py
@@ -13,12 +13,10 @@
 KEY_VALUE_HEADS = 3
 HEAD_SIZE = 64
 LAYERS = 2
-KV_WIDTH = 2 * KEY_VALUE_HEADS * HEAD_SIZE
 
 EPSILON = 1e-05
 THETA = 100000.0
 MASKED = -1e30
-HIGHEST = lax.Precision.HIGHEST
 MESH = pl.DeviceIdType.MESH
 RING = 4
 
@@ -143,9 +141,12 @@
     )
 
 
-def attend_group(g, own, kv, queries, flags, tall, out, lse, keys, values, scores, rows):
+def attend_group(
+    g, own, kv, queries, flags, tall, out, lse, keys, values, scores, rows, between
+):
     pack_all(g, kv, own, tall, keys, values)
     score_all(keys, queries[g], scores)
+    between()
     rows[...] = jnp.full(rows.shape, MASKED, jnp.float32)
 
     for t in range(TILES):
@@ -363,95 +364,17 @@
     return begin, forward, arrive, finish
 
 
-def forward_kernel(
-    own, queries, flags, tall, source, out, lse, kv, whole,
-    keys, values, scores, rows, *sems
-):
-    me = place()
-    greet_all(me)
-    begin, forward, arrive, finish = row_gather(me, own, kv, *sems[:5])
-    w_begin, w_forward, w_exchange, w_finish = weight_gather(me, source, whole, *sems[5:])
-    for g in range(3):
-        begin(g)
-    w_begin()
-    for g in range(3):
-        forward(g)
-    w_forward(1)
-
-    def one(g, carry):
-        arrive(g)
-
-        @pl.when(g == 1)
-        def _():
-            w_forward(2)
-
-        attend_group(g, own, kv, queries, flags, tall, out, lse, keys, values, scores, rows)
-        return carry
-
-    lax.fori_loop(0, 3, one, 0)
-    w_exchange()
-    for g in range(3):
-        finish(g)
-    w_finish()
-
-
-def attention_forward(own, queries, flags, source):
-    vmem = pl.BlockSpec(memory_space=pltpu.VMEM)
-    hbm = pl.BlockSpec(memory_space=pl.ANY)
-    return pl.pallas_call(
-        forward_kernel,
-        out_shape=(
-            jax.ShapeDtypeStruct((3, 64, LANES), jnp.float32),
-            jax.ShapeDtypeStruct((3, 8, LANES), jnp.float32),
-            jax.ShapeDtypeStruct((3, 4, 4, 2, 128, 128), jnp.bfloat16),
-            WHOLE,
-        ),
-        in_specs=[vmem, vmem, vmem, vmem, hbm],
-        out_specs=(vmem, vmem, vmem, hbm),
-        scratch_shapes=[
-            pltpu.VMEM((64 * TILES, 256), jnp.bfloat16),
-            pltpu.VMEM((64 * TILES, 256), jnp.bfloat16),
-            pltpu.VMEM((64 * TILES, LANES), jnp.float32),
-            pltpu.VMEM((40, LANES), jnp.float32),
-            pltpu.SemaphoreType.DMA((3, 2, 2, 3)),
-            pltpu.SemaphoreType.DMA((3, 2, 2, 3)),
-            pltpu.SemaphoreType.DMA((3, 2, 4)),
-            pltpu.SemaphoreType.DMA((3, 2, 4)),
-            pltpu.SemaphoreType.DMA((3,)),
-        ] + WEIGHT_GATHER_SEMS,
-        compiler_params=pltpu.CompilerParams(
-            collective_id=2, has_side_effects=True, vmem_limit_bytes=40 * 2**20
-        ),
-        name="attention_forward",
-    )(own, queries, *flags, source)
-
-
 def weight_reduce(
-    me, planes, out, grads, halves, first, landed_a, sum_a, landed_b, sum_b, landed_c,
+    me, out, grads, halves, landed_a, sum_a, landed_b, sum_b, landed_c,
     swap_sends, swap_recvs, sends, recvs,
 ):
     axes = ((2, 1, 0), (0, 2, 1), (1, 0, 2))
 
-    def outer(left, right):
-        return dot_rows(left, right).astype(jnp.bfloat16)
-
     def swap(y):
         return pltpu.make_async_remote_copy(
             src_ref=grads.at[y, :, :, 1 - me[3]], dst_ref=halves.at[y],
             send_sem=swap_sends.at[y], recv_sem=swap_recvs.at[y],
             device_id=device(*sibling(me)), device_id_type=MESH)
-
-    def multiply(y):
-        at = 0
-        for left, right in planes[y]:
-            flat = outer(left[...], right[...])
-            count = flat.shape[0] // 48
-            cut = flat.reshape(count, 48, MODEL_WIDTH)
-            for i in range(count):
-                j = at + i
-                grads[y, j // 8, (j // 2) % 4, j % 2] = cut[i]
-            at += count
-        swap(y).start()
 
     def copy(stage, src, dst, k, s, peer):
         return pltpu.make_async_remote_copy(
@@ -465,7 +388,7 @@
         if stage == 0:
             index = [slice(None)] * 3
             index[axis] = peer[axis]
-            return copy(0, first.at[tuple(index) + (pl.ds(16 * k, 16),)], landed_a.at[k, s - 1], k, s, peer)
+            return copy(0, halves.at[tuple(index) + (pl.ds(16 * k, 16),)], landed_a.at[k, s - 1], k, s, peer)
         if stage == 1:
             index = [slice(None)] * 2
             index[sorted(axes[k][1:]).index(axis)] = peer[axis]
@@ -476,7 +399,7 @@
         swap(y).wait_recv()
         for x in range(4):
             for z in range(4):
-                first[y, x, z] = (
+                halves[y, x, z] = (
                     grads[y, x, z, me[3]].astype(jnp.float32) + halves[y, x, z].astype(jnp.float32)
                 ).astype(jnp.bfloat16)
 
@@ -494,7 +417,7 @@
                 for j in range(4):
                     at = [i, j]
                     at.insert(axis, me[axis])
-                    total = first[tuple(at) + (pl.ds(16 * k, 16),)].astype(jnp.float32)
+                    total = halves[tuple(at) + (pl.ds(16 * k, 16),)].astype(jnp.float32)
                     for s in range(3):
                         total = total + landed_a[k, s, i, j].astype(jnp.float32)
                     sum_a[k, i, j] = total.astype(jnp.bfloat16)
@@ -516,7 +439,7 @@
             for s in (2, 1, 3):
                 send(2, k, s).start()
 
-    def finish():
+    def finish(planes):
         for k in range(3):
             for s in (1, 3, 2):
                 send(2, k, s).wait_recv()
@@ -524,21 +447,20 @@
             for s in range(3):
                 total = total + landed_c[k, s].astype(jnp.float32)
             out[pl.ds(16 * k, 16)] = total
-        for y in sorted(planes):
+        for y in planes:
             swap(y).wait_send()
         for stage in range(3):
             for k in range(3):
                 for s in (1, 2, 3):
                     send(stage, k, s).wait_send()
 
-    return multiply, halve, begin, second, third, finish
+    return swap, halve, begin, second, third, finish
 
 
 def weight_reduce_scratch():
     bf, w = jnp.bfloat16, MODEL_WIDTH
     return [
         pltpu.VMEM((4, 4, 4, 2, 48, w), bf),
-        pltpu.VMEM((4, 4, 4, 48, w), bf),
         pltpu.VMEM((4, 4, 4, 48, w), bf),
         pltpu.VMEM((3, 3, 4, 4, 16, w), bf),
         pltpu.VMEM((3, 4, 4, 16, w), bf),
@@ -553,7 +475,7 @@
 
 
 def row_reduce(
-    me, terms, out, halves, first, landed_a, sum_a, landed_b, swap_sends, swap_recvs, sends, recvs
+    me, terms, out, halves, landed_a, sum_a, landed_b, swap_sends, swap_recvs, sends, recvs
 ):
     axes = ((2, 1), (1, 2))
 
@@ -569,7 +491,7 @@
         if stage == 0:
             index = [slice(None)] * 2
             index[axis - 1] = peer[axis]
-            src = first.at[(g,) + tuple(index) + (pl.ds(64 * k, 64),)]
+            src = halves.at[(g,) + tuple(index) + (pl.ds(64 * k, 64),)]
             dst = landed_a.at[g, k, s - 1]
         else:
             src = sum_a.at[g, k, peer[axis]]
@@ -586,7 +508,7 @@
         swap(g).wait_recv()
         for x in range(4):
             for z in range(4):
-                first[g, x, z] = (
+                halves[g, x, z] = (
                     terms[g, x, z, me[3]].astype(jnp.float32) + halves[g, x, z].astype(jnp.float32)
                 ).astype(jnp.bfloat16)
         for s in (2, 1, 3):
@@ -601,7 +523,7 @@
             for i in range(4):
                 at = [i]
                 at.insert(axis - 1, me[axis])
-                total = first[(g,) + tuple(at) + (pl.ds(64 * k, 64),)].astype(jnp.float32)
+                total = halves[(g,) + tuple(at) + (pl.ds(64 * k, 64),)].astype(jnp.float32)
                 for s in range(3):
                     total = total + landed_a[g, k, s, i].astype(jnp.float32)
                 sum_a[g, k, i] = total.astype(jnp.bfloat16)
@@ -630,7 +552,6 @@
 def row_reduce_scratch():
     bf = jnp.bfloat16
     return [
-        pltpu.VMEM((3, 4, 4, 128, 128), bf),
         pltpu.VMEM((3, 4, 4, 128, 128), bf),
         pltpu.VMEM((3, 2, 3, 4, 64, 128), bf),
         pltpu.VMEM((3, 2, 4, 64, 128), bf),
@@ -642,31 +563,266 @@
     ]
 
 
-def backward_kernel(shape, *refs):
-    count = 1 + max(i for plane in shape.values() for pair in plane for i in pair)
-    kv, own, queries, grads, lse, inner, flags, tall = refs[:8]
-    arrays = refs[8 : 8 + count]
-    dq, sums, owned = refs[8 + count : 11 + count]
-    keys, values, scores, lse_rows, inner_rows, dkv = refs[11 + count : 17 + count]
-    row_refs = refs[17 + count : 26 + count]
-    weight_refs = refs[26 + count :]
+def left_lanes():
+    return lax.broadcasted_iota(jnp.int32, (128, 128), 1) < 64
+
+
+def swapped(tile):
+    low = lax.broadcasted_iota(jnp.int32, tile.shape, 1) % 64 < 32
+    return jnp.where(low, pltpu.roll(tile, 96, 1), pltpu.roll(tile, 32, 1))
+
+
+def spread_tile(spots, tile, j):
+    other = pltpu.roll(tile, 64, 1)
+    left = left_lanes()
+    for i in range(2):
+        head = 2 * j + i
+        if head >= QUERY_HEADS:
+            continue
+        a = jnp.where(left, tile if i == 0 else other, 0.0).astype(jnp.bfloat16)
+        b = jnp.where(left, 0.0, other if i == 0 else tile).astype(jnp.bfloat16)
+        g, at = head // 3, 128 * (head % 3)
+        spots[g, at : at + 64, :128] = b[:64]
+        spots[g, at : at + 64, 128:] = a[64:]
+        spots[g, at + 64 : at + 128, :128] = a[64:]
+        spots[g, at + 64 : at + 128, 128:] = jnp.zeros((64, 128), jnp.bfloat16)
+
+
+def group_weights(first, g):
+    return jnp.concatenate(
+        [first[0, 576 + 64 * g : 640 + 64 * g], first[0, 768 + 64 * g : 832 + 64 * g]], axis=0
+    )
+
+
+def inverse_root(values):
+    return lax.rsqrt(jnp.mean(values * values, axis=-1, keepdims=True) + EPSILON)
+
+
+def forward_kernel(
+    hidden, planes, gains, cosine, sine, flags, tall, source,
+    n1, queries, own, kv, turned, lse, mixed, middle, n2, gate, up, product, result, whole,
+    keys, values, scores, rows, first, first_sem, *sems
+):
     me = place()
+    load = pltpu.make_async_copy(planes.at[pl.ds(0, 1)], first, first_sem)
+    load.start()
     greet_all(me)
-    planes = {
-        y: [(arrays[i], arrays[j]) for i, j in pairs] for y, pairs in shape.items()
-    }
+    load.wait()
+    begin, forward, arrive, finish = row_gather(me, own, kv, *sems[:5])
+    w_begin, w_forward, w_exchange, w_finish = weight_gather(me, source, whole, *sems[5:])
+    left = left_lanes()
+    x = hidden[...]
+    normed = (x * inverse_root(x) * gains[:1]).astype(jnp.bfloat16)
+    n1[...] = normed
+    cos, sin = cosine[...], sine[...]
+    for g in range(3):
+        tile = dot_cols(normed, group_weights(first, g))
+        tile = tile * jnp.where(left, cos, 1.0) + swapped(tile) * jnp.where(left, sin, 0.0)
+        own[g] = tile.astype(jnp.bfloat16)
+        begin(g)
+    w_begin()
+    for j in range(5):
+        tile = dot_cols(normed, first[0, 128 * j : 128 * j + 128])
+        tile = (tile * cos + swapped(tile) * sin) * HEAD_SIZE ** (-0.5)
+        spread_tile(queries, tile, j)
+    for g in range(3):
+        forward(g)
+    w_forward(1)
+
+    def one(g, carry):
+        arrive(g)
+
+        def between():
+            @pl.when(g == 0)
+            def _():
+                w_forward(2)
+
+        attend_group(
+            g, own, kv, queries, flags, tall, turned, lse, keys, values, scores, rows, between
+        )
+        return carry
+
+    lax.fori_loop(0, 3, one, 0)
+    for g in range(3):
+        for h in range(3):
+            mixed[64 * (3 * g + h) : 64 * (3 * g + h) + 64] = turned[
+                g, :, 128 * h : 128 * h + 128
+            ].astype(jnp.bfloat16)
+    mid = x + dot_rows(mixed[...], first[0, 960:1536])
+    middle[...] = mid
+    normed = (mid * inverse_root(mid) * gains[1:2]).astype(jnp.bfloat16)
+    n2[...] = normed
+    w_exchange()
+    for g in range(3):
+        finish(g)
+    w_finish()
+    total = mid
+    for i in range(4):
+        part = pl.ds(384 * i, 384)
+        gate_values = dot_cols(normed, whole[1, i].reshape(384, MODEL_WIDTH))
+        up_values = dot_cols(normed, whole[2, i].reshape(384, MODEL_WIDTH))
+        rounded = (gate_values * jax.nn.sigmoid(gate_values) * up_values).astype(jnp.bfloat16)
+        gate[:, part] = gate_values
+        up[:, part] = up_values
+        product[:, part] = rounded
+        total = total + jnp.dot(
+            rounded, whole[3, i].reshape(384, MODEL_WIDTH), preferred_element_type=jnp.float32
+        )
+    result[...] = total
+
+
+ROWS_F32 = jax.ShapeDtypeStruct((128, MODEL_WIDTH), jnp.float32)
+ROWS_BF16 = jax.ShapeDtypeStruct((128, MODEL_WIDTH), jnp.bfloat16)
+TURNED_BF16 = jax.ShapeDtypeStruct((MODEL_WIDTH, 128), jnp.bfloat16)
+WIDE_F32 = jax.ShapeDtypeStruct((128, FEEDFORWARD_SIZE), jnp.float32)
+WIDE_BF16 = jax.ShapeDtypeStruct((128, FEEDFORWARD_SIZE), jnp.bfloat16)
+VMEM_SPEC = pl.BlockSpec(memory_space=pltpu.VMEM)
+HBM_SPEC = pl.BlockSpec(memory_space=pl.ANY)
+
+
+def layer_forward(hidden, planes, gains, turns, flags, source):
+    outs = pl.pallas_call(
+        forward_kernel,
+        out_shape=(
+            ROWS_BF16,
+            jax.ShapeDtypeStruct((3, LANES, 256), jnp.bfloat16),
+            jax.ShapeDtypeStruct((3, 128, 128), jnp.bfloat16),
+            jax.ShapeDtypeStruct((3, 4, 4, 2, 128, 128), jnp.bfloat16),
+            jax.ShapeDtypeStruct((3, 64, LANES), jnp.float32),
+            jax.ShapeDtypeStruct((3, 8, LANES), jnp.float32),
+            TURNED_BF16, ROWS_F32, ROWS_BF16, WIDE_F32, WIDE_F32, WIDE_BF16, ROWS_F32, WHOLE,
+        ),
+        in_specs=[VMEM_SPEC, HBM_SPEC] + [VMEM_SPEC] * 5 + [HBM_SPEC],
+        out_specs=(VMEM_SPEC,) * 14,
+        scratch_shapes=[
+            pltpu.VMEM((64 * TILES, 256), jnp.bfloat16),
+            pltpu.VMEM((64 * TILES, 256), jnp.bfloat16),
+            pltpu.VMEM((64 * TILES, LANES), jnp.float32),
+            pltpu.VMEM((40, LANES), jnp.float32),
+            pltpu.VMEM((1, 1536, MODEL_WIDTH), jnp.bfloat16),
+            pltpu.SemaphoreType.DMA,
+            pltpu.SemaphoreType.DMA((3, 2, 2, 3)),
+            pltpu.SemaphoreType.DMA((3, 2, 2, 3)),
+            pltpu.SemaphoreType.DMA((3, 2, 4)),
+            pltpu.SemaphoreType.DMA((3, 2, 4)),
+            pltpu.SemaphoreType.DMA((3,)),
+        ] + WEIGHT_GATHER_SEMS,
+        compiler_params=pltpu.CompilerParams(
+            collective_id=6 + planes.shape[0], has_side_effects=True, vmem_limit_bytes=48 * 2**20
+        ),
+        name="layer_forward",
+    )(hidden, planes, gains, *turns[:2], *flags, source)
+    return outs[:-2], outs[-2], outs[-1].reshape(4, 1536, MODEL_WIDTH)
+
+
+def norm_back(grad_normed, values, gain):
+    inverse = inverse_root(values)
+    unit = values * inverse
+    grad_gain = jnp.sum(grad_normed * unit, axis=0, keepdims=True)
+    scaled = grad_normed * gain
+    grad_values = inverse * (
+        scaled - unit * jnp.mean(scaled * unit, axis=-1, keepdims=True)
+    )
+    return grad_values, grad_gain
+
+
+def products_first(gq, gkv, mixed, n1, gb):
+    parts = [jnp.dot(gq[...], n1[...], preferred_element_type=jnp.float32)]
+    both = [dot_rows(gkv[g], n1[...]) for g in range(3)]
+    parts.append(jnp.concatenate([m[:64] for m in both], axis=0))
+    parts.append(jnp.concatenate([m[64:] for m in both], axis=0))
+    parts.append(jnp.dot(mixed[...], gb[...], preferred_element_type=jnp.float32))
+    return [
+        p.astype(jnp.bfloat16).reshape(p.shape[0] // 48, 48, MODEL_WIDTH) for p in parts
+    ]
+
+
+def backward_kernel(extra_count, *refs):
+    (
+        grad_result, hidden, planes, rest, gains, cosine, sine, cosine_t, sine_t, flags, tall,
+        n1, queries, own, kv, turned, lse, mixed, middle, n2, gate, up, product,
+    ) = refs[:23]
+    more = refs[23 : 23 + extra_count]
+    grad_hidden, owned, gq, gkv, gb, gain_terms = refs[23 + extra_count : 29 + extra_count]
+    (
+        keys, values, scores, lse_rows, inner_rows, dkv, spots, inner, dq, sums, ggate, gup,
+        first, whole, load_sems,
+    ) = refs[29 + extra_count : 44 + extra_count]
+    row_refs = refs[44 + extra_count : 52 + extra_count]
+    weight_refs = refs[52 + extra_count :]
+    me = place()
+    loads = [
+        pltpu.make_async_copy(rest.at[pl.ds(1, 3)], whole, load_sems.at[0]),
+        pltpu.make_async_copy(planes.at[pl.ds(0, 1)], first, load_sems.at[1]),
+    ]
+    for load in loads:
+        load.start()
+    greet_all(me)
+    for load in loads:
+        load.wait()
     begin, second, third, finish, drain = row_reduce(me, dkv, sums, *row_refs)
-    multiply, halve, w_begin, w_second, w_third, w_finish = weight_reduce(
-        me, planes, owned, *weight_refs
+    swap, halve, w_begin, w_second, w_third, w_finish = weight_reduce(
+        me, owned, *weight_refs
     )
-    first_sums = weight_refs[2]
-    order = sorted(planes, key=lambda y: (y == 0, y))
-    for y in order:
-        multiply(y)
+    grads, halves = weight_refs[0], weight_refs[1]
+    order = (1, 2, 3, 0) if more else (1, 2, 3)
+
+    gr = grad_result[...]
+    gd = gr.astype(jnp.bfloat16)
+    normed = n2[...]
+    grad_normed = jnp.zeros((128, MODEL_WIDTH), jnp.float32)
+    for i in range(4):
+        part = pl.ds(384 * i, 384)
+        grad_product = dot_cols(gd, whole[2, i])
+        gate_values, up_values = gate[:, part], up[:, part]
+        s = jax.nn.sigmoid(gate_values)
+        gg = (grad_product * up_values * (s * (1.0 + gate_values * (1.0 - s)))).astype(jnp.bfloat16)
+        gu = (grad_product * (gate_values * s)).astype(jnp.bfloat16)
+        ggate[:, part] = gg
+        gup[:, part] = gu
+        grad_normed = grad_normed + jnp.dot(
+            gg, whole[0, i], preferred_element_type=jnp.float32
+        ) + jnp.dot(
+            gu, whole[1, i], preferred_element_type=jnp.float32
+        )
+    for y, source, right in ((1, ggate, normed), (2, gup, normed), (3, product, gd)):
+        for i in range(4):
+            flat = dot_rows(source[:, 384 * i : 384 * i + 384], right).astype(jnp.bfloat16)
+            grads[y, i] = flat.reshape(4, 2, 48, MODEL_WIDTH)
+        swap(y).start()
+    grad_middle, grad_gain = norm_back(grad_normed, middle[...], gains[1:2])
+    gain_terms[...] = jnp.zeros(gain_terms.shape, jnp.float32)
+    gain_terms[1:2] = grad_gain
+    grad_middle = grad_middle + gr
+    branch = grad_middle.astype(jnp.bfloat16)
+    gb[...] = branch
+    if more:
+        at = 0
+        for cut in products_first(*more):
+            for i in range(cut.shape[0]):
+                j = at + i
+                grads[0, j // 8, (j // 2) % 4, j % 2] = cut[i]
+            at += cut.shape[0]
+        swap(0).start()
+    for j in range(5):
+        width = min(128, 576 - 128 * j)
+        tile = dot_cols(branch, first[0, 960 + 128 * j : 960 + 128 * j + width])
+        if width < 128:
+            tile = jnp.concatenate([tile, jnp.zeros((128, 128 - width), jnp.float32)], axis=1)
+        spread_tile(spots, tile, j)
+    for g in range(3):
+        for h in range(3):
+            at = 64 * (3 * g + h)
+            grad_turned = dot_cols(first[0, 960 + at : 1024 + at], branch)
+            grad_turned = grad_turned.astype(jnp.bfloat16).astype(jnp.float32)
+            row = jnp.sum(
+                turned[g, :, 128 * h : 128 * h + 128] * grad_turned, axis=0, keepdims=True
+            )
+            inner[g, :, 128 * h : 128 * h + 128] = jnp.broadcast_to(row, (8, 128))
 
     def one(g, carry):
         attend_back_group(
-            g, me, kv, own, queries, grads, lse, inner, flags, tall, dq, dkv,
+            g, me, kv, own, queries, spots, lse, inner, flags, tall, dq, dkv,
             keys, values, scores, lse_rows, inner_rows,
         )
         begin(g)
@@ -675,8 +831,8 @@
         def _():
             for y in order:
                 halve(y)
-            if 0 not in planes:
-                first_sums[0] = jnp.zeros(first_sums.shape[1:], jnp.bfloat16)
+            if not more:
+                halves[0] = jnp.zeros(halves.shape[1:], jnp.bfloat16)
             w_begin()
 
         @pl.when(g == 1)
@@ -696,24 +852,46 @@
     third(1)
     w_third()
     third(2)
-    w_finish()
+    for g in range(3):
+        for h in range(3):
+            turn = dq[g, :, 128 * h : 128 * h + 128] * HEAD_SIZE ** (-0.5)
+            a, b = turn[:32], turn[32:]
+            at = 64 * (3 * g + h)
+            gq[at : at + 32] = (a * cosine_t[...] + b * sine_t[...]).astype(jnp.bfloat16)
+            gq[at + 32 : at + 64] = (b * cosine_t[...] - a * sine_t[...]).astype(jnp.bfloat16)
+    grad_normed = dot_rows(gq[...], first[0, :576])
+    left = left_lanes()
+    cos, sin = jnp.where(left, cosine[...], 1.0), jnp.where(left, sine[...], 0.0)
+    w_finish(order)
     for g in range(3):
         finish(g)
+        tile = sums[g]
+        tile = (tile * cos - swapped(tile) * sin).astype(jnp.bfloat16)
+        gkv[g] = tile
+        grad_normed = grad_normed + jnp.dot(
+            tile, group_weights(first, g), preferred_element_type=jnp.float32
+        )
+    grad_values, grad_gain = norm_back(grad_normed, hidden[...], gains[:1])
+    gain_terms[:1] = grad_gain
+    grad_hidden[...] = grad_values + grad_middle
     for g in range(3):
         drain(g)
 
 
-def attention_backward(collective_id, shape, kv, own, queries, grads, lse, inner, flags, arrays):
-    vmem = pl.BlockSpec(memory_space=pltpu.VMEM)
+def layer_backward(collective_id, grad_result, hidden, first, whole, gains, turns, flags, kept, more):
+    rest = whole.reshape(4, 4, 384, MODEL_WIDTH)
     return pl.pallas_call(
-        functools.partial(backward_kernel, shape),
+        functools.partial(backward_kernel, len(more)),
         out_shape=(
-            jax.ShapeDtypeStruct((3, 64, LANES), jnp.float32),
-            jax.ShapeDtypeStruct((3, 128, 128), jnp.float32),
+            ROWS_F32,
             jax.ShapeDtypeStruct((48, MODEL_WIDTH), jnp.float32),
+            TURNED_BF16,
+            jax.ShapeDtypeStruct((3, 128, 128), jnp.bfloat16),
+            ROWS_BF16,
+            jax.ShapeDtypeStruct((8, MODEL_WIDTH), jnp.float32),
         ),
-        in_specs=[vmem] * (8 + len(arrays)),
-        out_specs=(vmem,) * 3,
+        in_specs=[VMEM_SPEC] * 2 + [HBM_SPEC] * 2 + [VMEM_SPEC] * (19 + len(more)),
+        out_specs=(VMEM_SPEC,) * 6,
         scratch_shapes=[
             pltpu.VMEM((64 * TILES, 256), jnp.bfloat16),
             pltpu.VMEM((64 * TILES, 256), jnp.bfloat16),
@@ -721,12 +899,21 @@
             pltpu.VMEM((40, LANES), jnp.float32),
             pltpu.VMEM((40, LANES), jnp.float32),
             pltpu.VMEM((3, 4, 4, 2, 128, 128), jnp.bfloat16),
+            pltpu.VMEM((3, LANES, 256), jnp.bfloat16),
+            pltpu.VMEM((3, 8, LANES), jnp.float32),
+            pltpu.VMEM((3, 64, LANES), jnp.float32),
+            pltpu.VMEM((3, 128, 128), jnp.float32),
+            pltpu.VMEM((128, FEEDFORWARD_SIZE), jnp.bfloat16),
+            pltpu.VMEM((128, FEEDFORWARD_SIZE), jnp.bfloat16),
+            pltpu.VMEM((1, 1536, MODEL_WIDTH), jnp.bfloat16),
+            pltpu.VMEM((3, 4, 384, MODEL_WIDTH), jnp.bfloat16),
+            pltpu.SemaphoreType.DMA((2,)),
         ] + row_reduce_scratch() + weight_reduce_scratch(),
         compiler_params=pltpu.CompilerParams(
-            collective_id=collective_id, has_side_effects=True, vmem_limit_bytes=58 * 2**20
+            collective_id=collective_id, has_side_effects=True, vmem_limit_bytes=60 * 2**20
         ),
-        name="attention_backward",
-    )(kv, own, queries, grads, lse, inner, *flags, *arrays)
+        name="layer_backward",
+    )(grad_result, hidden, first, rest, gains, *turns, *flags, *kept, *more)
 
 
 HALF_ROWS = ((0, 32), (32, 16))
@@ -882,7 +1069,7 @@
 
 
 def reduce_last_kernel(
-    gq, gk, gv, mixed, n1, gb, gains, out, gains_out,
+    gq, gkv, mixed, n1, gb, gains, out, gains_out,
     grads, halves, first, landed_a, sum_a, landed_b, sum_b, landed_y, gain_in, gain_sum,
     swap_sends, swap_recvs, sends, recvs, y_sends, y_recvs, gain_sends, gain_recvs
 ):
@@ -938,10 +1125,8 @@
     gain_sum[0] = gains[...]
     gain_copy(0, 1, sibling(me)).start()
     at = 0
-    for left, right in ((gq, n1), (gk, n1), (gv, n1), (mixed, gb)):
-        flat = dot_rows(left[...], right[...]).astype(jnp.bfloat16)
-        amount = flat.shape[0] // 48
-        cut = flat.reshape(amount, 48, MODEL_WIDTH)
+    for cut in products_first(gq, gkv, mixed, n1, gb):
+        amount = cut.shape[0]
         for i in range(amount):
             j = at + i
             grads[j // 8, (j // 2) % 4, j % 2] = cut[i]
@@ -1013,7 +1198,7 @@
             jax.ShapeDtypeStruct((48, w), jnp.float32),
             jax.ShapeDtypeStruct(gains.shape, jnp.float32),
         ),
-        in_specs=[vmem] * 7,
+        in_specs=[vmem] * 6,
         out_specs=(vmem, vmem),
         scratch_shapes=[
             pltpu.VMEM((4, 4, 2, 48, w), bf),
@@ -1024,8 +1209,8 @@
             pltpu.VMEM((3, 48, w), bf),
             pltpu.VMEM((48, w), bf),
             pltpu.VMEM((3, 48, w), bf),
-            pltpu.VMEM((4, 3, rows, 128), jnp.float32),
-            pltpu.VMEM((4, rows, 128), jnp.float32),
+            pltpu.VMEM((4, 3, rows, w), jnp.float32),
+            pltpu.VMEM((4, rows, w), jnp.float32),
             pltpu.SemaphoreType.DMA((4,)),
             pltpu.SemaphoreType.DMA((4,)),
             pltpu.SemaphoreType.DMA((2, 2, 3)),
@@ -1042,153 +1227,14 @@
     )(*arrays, gains)
 
 
-def rotation_parts(places, heads):
-    feature_width = heads * HEAD_SIZE
-    half_size = HEAD_SIZE // 2
-    feature_index = jnp.arange(feature_width)
-    within = feature_index % HEAD_SIZE
-    pair_index = within % half_size
-    frequency = 1.0 / THETA ** ((2 * pair_index).astype(jnp.float32) / HEAD_SIZE)
+def turn_tables(places):
+    half = HEAD_SIZE // 2
+    frequency = 1.0 / THETA ** (2 * jnp.arange(half).astype(jnp.float32) / HEAD_SIZE)
     phases = places.astype(jnp.float32)[:, None] * frequency[None, :]
-    head_of = feature_index // HEAD_SIZE
-    same_head = head_of[:, None] == head_of[None, :]
-    lower_target = within[None, :] < half_size
-    from_upper = (within[:, None] == within[None, :] + half_size) & lower_target
-    from_lower = (within[:, None] + half_size == within[None, :]) & jnp.logical_not(lower_target)
-    swapper = jnp.where(
-        same_head & from_upper, -1.0, jnp.where(same_head & from_lower, 1.0, 0.0)
-    ).astype(jnp.float32)
-    return (jnp.cos(phases), jnp.sin(phases), swapper)
-
-
-def apply_rotation(values, parts):
-    cosine_wide, sine_wide, swapper = parts
-    swapped = jnp.dot(values, swapper, precision=HIGHEST)
-    return values * cosine_wide + swapped * sine_wide
-
-
-def inverse_rotation(values, parts):
-    cosine_wide, sine_wide, swapper = parts
-    swapped = jnp.dot(values, swapper, precision=HIGHEST)
-    return values * cosine_wide - swapped * sine_wide
-
-
-def rms_inverse(values):
-    return lax.rsqrt(jnp.mean(values * values, -1, keepdims=True) + EPSILON)
-
-
-def norm_backward(grad_normed, values, inverse, gain):
-    unit_rows = values * inverse
-    grad_gain = jnp.sum(grad_normed * unit_rows, 0)
-    scaled = grad_normed * gain.astype(jnp.float32)
-    grad_values = inverse * (scaled - unit_rows * jnp.mean(scaled * unit_rows, -1, keepdims=True))
-    return (grad_values, grad_gain)
-
-
-def by_group(rows):
-    return rows.reshape(128, QUERY_HEADS, HEAD_SIZE).transpose(1, 0, 2).reshape(3, LANES, HEAD_SIZE)
-
-
-def spread(rows):
-    parts = rows.reshape(128, QUERY_HEADS, HEAD_SIZE).transpose(1, 0, 2)
-    lo, hi = parts[:, :64], parts[:, 64:]
-    zero = jnp.zeros_like(lo)
-    top = jnp.concatenate([zero, lo, hi, zero], -1)
-    low = jnp.concatenate([hi, zero, zero, zero], -1)
-    return jnp.concatenate([top, low], 1).reshape(3, LANES, 256)
-
-
-def by_token(turned):
-    return turned.reshape(3, HEAD_SIZE, 3, 128).transpose(3, 0, 2, 1).reshape(128, MODEL_WIDTH)
-
-
-def paired(keys, values):
-    both = jnp.stack([keys.reshape(128, 3, 64), values.reshape(128, 3, 64)], 2)
-    return both.reshape(128, 3, 128).transpose(1, 0, 2)
-
-
-def layer_forward(hidden, first, gains, flags, source, query_parts, key_parts):
-    query_t, key_t, value_t, w_out = jnp.split(first, (576, 768, 960), axis=0)
-    inverse_one = rms_inverse(hidden)
-    normed_one = (hidden * inverse_one * gains[:MODEL_WIDTH].astype(jnp.float32)).astype(jnp.bfloat16)
-    query_rows = apply_rotation(dot_cols(normed_one, query_t), query_parts).astype(jnp.bfloat16)
-    key_rows = apply_rotation(dot_cols(normed_one, key_t), key_parts).astype(jnp.bfloat16)
-    value_rows = dot_cols(normed_one, value_t).astype(jnp.bfloat16)
-    own = paired(key_rows, value_rows)
-    queries = spread(query_rows * jnp.bfloat16(HEAD_SIZE ** (-0.5)))
-    turned, lse, kv, whole = attention_forward(own, queries, flags, source)
-    whole = whole.reshape(4, 1536, MODEL_WIDTH)
-    gate_t, up_t, w_down = whole[1], whole[2], whole[3]
-    mixed = by_token(turned).astype(jnp.bfloat16)
-    middle = hidden + jnp.dot(mixed, w_out, preferred_element_type=jnp.float32)
-    inverse_two = rms_inverse(middle)
-    normed_two = (middle * inverse_two * gains[MODEL_WIDTH:].astype(jnp.float32)).astype(jnp.bfloat16)
-    gate_values = dot_cols(normed_two, gate_t)
-    up_values = dot_cols(normed_two, up_t)
-    product = (jax.nn.silu(gate_values) * up_values).astype(jnp.bfloat16)
-    result = middle + jnp.dot(product, w_down, preferred_element_type=jnp.float32)
-    kept = (
-        hidden, inverse_one, normed_one, queries, own, kv, turned, lse, mixed,
-        middle, inverse_two, normed_two, gate_values, up_values, product,
-        (query_t, key_t, value_t, w_out, gate_t, up_t, w_down),
+    cos, sin = jnp.cos(phases), jnp.sin(phases)
+    return (
+        jnp.concatenate([cos] * 4, 1), jnp.concatenate([-sin, sin] * 2, 1), cos.T, sin.T,
     )
-    return result, kept, whole[0]
-
-
-def layer_backward(grad_result, kept, gains, flags, more, query_parts, key_parts):
-    (
-        hidden, inverse_one, normed_one, queries, own, kv, turned, lse, mixed,
-        middle, inverse_two, normed_two, gate_values, up_values, product,
-        (query_t, key_t, value_t, w_out, gate_t, up_t, w_down),
-    ) = kept
-    grad_down = grad_result.astype(jnp.bfloat16)
-    grad_product = dot_cols(grad_down, w_down)
-    sigmoid_values = jax.nn.sigmoid(gate_values)
-    grad_gate = (
-        grad_product * up_values * (sigmoid_values * (1.0 + gate_values * (1.0 - sigmoid_values)))
-    ).astype(jnp.bfloat16)
-    grad_up = (grad_product * (gate_values * sigmoid_values)).astype(jnp.bfloat16)
-    grad_normed_two = jnp.dot(grad_gate, gate_t, preferred_element_type=jnp.float32) + jnp.dot(
-        grad_up, up_t, preferred_element_type=jnp.float32
-    )
-    grad_middle, grad_gain_two = norm_backward(
-        grad_normed_two, middle, inverse_two, gains[MODEL_WIDTH:]
-    )
-    grad_middle = grad_middle + grad_result
-    grad_branch = grad_middle.astype(jnp.bfloat16)
-    grad_mixed = dot_cols(grad_branch, w_out).astype(jnp.bfloat16)
-    inner = jnp.sum(
-        turned * by_group(grad_mixed).astype(jnp.float32).transpose(0, 2, 1), 1, keepdims=True
-    )
-    inner = jnp.broadcast_to(inner, (3, 8, LANES))
-    arrays = (grad_gate, grad_up, product, normed_two, grad_down)
-    shape = {1: ((0, 3),), 2: ((1, 3),), 3: ((2, 4),)}
-    if more is not None:
-        arrays = arrays + more
-        shape[0] = ((5, 9), (6, 9), (7, 9), (8, 10))
-    dq, sums, owned = attention_backward(
-        3 if more is None else 4, shape,
-        kv, own, queries, spread(grad_mixed), lse, inner, flags, arrays,
-    )
-    sums = sums.transpose(1, 0, 2).reshape(128, 3, 2, 64)
-    key_sums = sums[:, :, 0].reshape(128, 192)
-    value_sums = sums[:, :, 1].reshape(128, 192)
-    grad_query = by_token(dq) * HEAD_SIZE ** (-0.5)
-    grad_query = inverse_rotation(grad_query, query_parts).astype(jnp.bfloat16)
-    key_gradient = inverse_rotation(key_sums, key_parts).astype(jnp.bfloat16)
-    value_gradient = value_sums.astype(jnp.bfloat16)
-    grad_normed_one = (
-        jnp.dot(grad_query, query_t, preferred_element_type=jnp.float32)
-        + jnp.dot(key_gradient, key_t, preferred_element_type=jnp.float32)
-        + jnp.dot(value_gradient, value_t, preferred_element_type=jnp.float32)
-    )
-    grad_hidden, grad_gain_one = norm_backward(
-        grad_normed_one, hidden, inverse_one, gains[:MODEL_WIDTH]
-    )
-    grad_hidden = grad_hidden + grad_middle
-    gain_terms = jnp.concatenate([grad_gain_one, grad_gain_two, jnp.zeros(896, jnp.float32)])
-    left = (grad_query, key_gradient, value_gradient, mixed, normed_one, grad_branch)
-    return grad_hidden, owned, left, gain_terms.reshape(16, 128)
 
 
 def on_device(hidden_in, positions, params, gains, cotangent):
@@ -1200,16 +1246,17 @@
     def lo_first(rows):
         return jnp.where(turn, jnp.concatenate([rows[64:], rows[:64]], 0), rows)
 
-    places = lo_first(places)
     extra = jnp.concatenate(
         [jnp.pad(gains, ((0, 0), (0, 119))), jnp.full((14, 128), block, jnp.bfloat16)], 0
     )
     at_front = lax.axis_index("fsdp") == 0
     sources = (jnp.where(at_front, params[1], params[0]), params[1])
     first, extras = gather_first(params[0], extra)
-    first = first.reshape(1536, MODEL_WIDTH)
+    turns = turn_tables(lo_first(places))
+    firsts = [first.reshape(1, 1536, MODEL_WIDTH)]
     extras = extras.reshape(128, 16, 128)
-    gain_rows = [extras[:, layer, :9].reshape(-1) for layer in range(LAYERS)]
+    gain_rows = extras[:, :2, :9].astype(jnp.float32).transpose(1, 0, 2)
+    gain_rows = jnp.pad(gain_rows.reshape(LAYERS, 2, MODEL_WIDTH), ((0, 0), (0, 6), (0, 0)))
     blocks = lax.dynamic_slice(
         extras[:, 2, 0], (lax.axis_index("fsdp") * 32,), (32,)
     ).astype(jnp.int32)
@@ -1218,28 +1265,32 @@
         jnp.broadcast_to(flags[:, None], (40, LANES)),
         jnp.broadcast_to(flags[:, None, None], (40, 8, 128)),
     )
-    query_parts = rotation_parts(places, QUERY_HEADS)
-    key_parts = rotation_parts(places, KEY_VALUE_HEADS)
     hidden = lo_first(hidden_in[0]).astype(jnp.float32)
-    kept = []
+    inputs, kept, wholes = [], [], []
     for layer in range(LAYERS):
-        hidden, state, first = layer_forward(
-            hidden, first, gain_rows[layer], flags, sources[layer], query_parts, key_parts
+        inputs.append(hidden)
+        state, hidden, whole = layer_forward(
+            hidden, firsts[layer], gain_rows[layer], turns, flags, sources[layer]
         )
         kept.append(state)
+        wholes.append(whole)
+        firsts.append(whole)
     output_rows = lo_first(hidden.astype(jnp.bfloat16))
     grad_hidden = lo_first(cotangent[0]).astype(jnp.float32)
     owned = [None] * LAYERS
     gain_terms = [None] * LAYERS
-    left = None
+    left = ()
     for layer in reversed(range(LAYERS)):
-        grad_hidden, owned[layer], left, gain_terms[layer] = layer_backward(
-            grad_hidden, kept[layer], gain_rows[layer], flags, left, query_parts, key_parts
+        grad_hidden, owned[layer], gq, gkv, gb, gain_terms[layer] = layer_backward(
+            3 + layer, grad_hidden, inputs[layer], firsts[layer], wholes[layer],
+            gain_rows[layer], turns, flags, kept[layer], left,
         )
+        left = (gq, gkv, kept[layer][6], kept[layer][0], gb)
     last, gain_sums = reduce_last(left, jnp.concatenate(gain_terms, 0))
     owned = [jnp.where(at_front, last, owned[0]), jnp.where(at_front, owned[0], owned[1])]
     index = lax.axis_index("fsdp") * 32 + lax.axis_index("ctx")
-    owned_gains = lax.dynamic_slice(gain_sums.reshape(LAYERS, 2048), (0, index * 9), (LAYERS, 9))
+    gain_sums = gain_sums.reshape(LAYERS, 8, MODEL_WIDTH)[:, :2].reshape(LAYERS, 2 * MODEL_WIDTH)
+    owned_gains = lax.dynamic_slice(gain_sums, (0, index * 9), (LAYERS, 9))
     return (
         output_rows[None],
         lo_first(grad_hidden)[None],

time: 359 us -> 306 us (0.85); the launches traced: 352 us -> 303 us
  matrix products: 46.2 us -> 0 us
  Pallas kernels: 244 us -> 265 us
  local copies, waits for them, and re-layouts: 45.5 us -> 28.7 us
  other arithmetic: 11.3 us -> 5.99 us
    dot_general x36 -> x0, matrix products: 46.2 us -> none  [the longest x14 20.5 us: dot_cols(): lax.dot_general(left, right, (((1,), (1,)), ((), ())), preferred_element_...]
    pallas_call x4, Pallas kernels: 189 us -> 209 us  [the longest x2 114 us: layer_backward(): pl.pallas_call(functools.partial(backward_kernel, len(more)), out_shape=(...]
    slice x11 -> x2, local copies, waits for them, and re-layouts: 8.32 us -> 0.99 us  [the longest x1 0.99 us: on_device(): gain_rows = extras[:, :2, :9].astype(jnp.float32).transpose(1, 0, 2)]
    unnamed x241 -> x86, local copies, waits for them, and re-layouts: 16.2 us -> 22.7 us
    transpose x6 -> x0, local copies, waits for them, and re-layouts: 4.52 us -> none  [the longest x4 2.32 us: layer_backward(): by_group(grad_mixed).astype(jnp.float32).transpose(0, 2, 1)]
    concatenate x6 -> x0, local copies, waits for them, and re-layouts: 3.87 us -> none  [the longest x4 3.72 us: spread(): return jnp.concatenate([top, low], 1).reshape(3, LANES, 256)]
where the time goes in v2:
time: 306 us; the launch traced here: 303 us
  Pallas kernels  265 us (87%)
  local copies, waits for them, and re-layouts  28.7 us (9%)
  other arithmetic  5.99 us (2%)
  between operations  3.93 us (1%)
    pallas_call x2, Pallas kernels, layer_backward(): pl.pallas_call(functools.partial(backward_kernel, len(more)), out_shape=(...  114 us
    pallas_call x2, Pallas kernels, layer_forward(): pl.pallas_call(forward_kernel, out_shape=(ROWS_BF16, jax.ShapeDtypeStruct...  95.9 us
    pallas_call x1, Pallas kernels, gather_first(): pl.pallas_call(gather_first_kernel, out_shape=(jax.ShapeDtypeStruct((4, 4...  28.6 us
    pallas_call x1, Pallas kernels, reduce_last(): pl.pallas_call(reduce_last_kernel, out_shape=(jax.ShapeDtypeStruct((48, w...  26.6 us
    unnamed x86, local copies, waits for them, and re-layouts  22.7 us

profile of v2, /device:TPU:1, one launch (start us, length us, event | category | flops | bytes accessed | tf_op | source)
XLA Modules:
  0.0 303.2 jit_solution(6951813662777808896)
XLA Ops:
  0.7 1.1 copy.29
  4.4 1.1 copy.35
  5.5 0.8 fusion.1
  6.3 1.6 slice_bitcast_fusion.4
  7.9 1.3 fusion.5.extra
  9.2 28.6 %gather_first.1 = (bf16[4,4,2,48,576]{4,3,2,1,0:T(8,128)(2,1)}, bf16[4,4,4,2,16,128]{5,4,3,2,1,0:T(8,128)(2,1)}) custom-call(bf16[48,576]{1,0:T(8,128)(2,1)} %get-tuple-element.115.source, bf16[16,128]{1,0:T(8,128)(2,1)} %fusion.5.extra), custom_call_target="tpu_custom_call" | custom-call | tf_op jit(solution)/shard_map/gather_first/pallas_call | solution.py:1046
  37.7 1.0 slice.97
  39.6 1.1 slice.99
  41.1 48.1 %layer_forward.2 = (bf16[128,576]{1,0:T(8,128)(2,1)S(1)}, bf16[3,384,256]{2,1,0:T(8,128)(2,1)S(1)}, bf16[3,128,128]{2,1,0:T(8,128)(2,1)S(1)}, bf16[3,4,4,2,128,1...) custom-call(f32[128,576]{1,0:T(8,128)S(1)} %get-tuple-element.125.hi, ...), custom_call_target="tpu_custom_call" | custom-call | tf_op jit(solution)/shard_map/layer_forward/pallas_call | solution.py:684
  89.2 0.9 copy-done.6
  90.1 0.9 copy-done.7
  92.3 0.8 copy-done.16
  93.2 0.7 copy-done.18
  93.9 0.7 copy-done.20
  97.3 47.7 %layer_forward.3 = (bf16[128,576]{1,0:T(8,128)(2,1)S(1)}, bf16[3,384,256]{2,1,0:T(8,128)(2,1)S(1)}, bf16[3,128,128]{2,1,0:T(8,128)(2,1)S(1)}, bf16[3,4,4,2,128,1...) custom-call(f32[128,576]{1,0:T(8,128)S(1)} %get-tuple-element.50.hid, ...), custom_call_target="tpu_custom_call" | custom-call | tf_op jit(solution)/shard_map/layer_forward/pallas_call | solution.py:684
  145.1 0.9 copy-done.8
  146.0 0.9 copy-done.9
  148.2 0.8 copy-done.17
  149.0 0.8 copy-done.19
  149.8 0.7 copy-done.21
  153.2 0.8 copy.38
  154.0 0.8 multiply_sine_fusion.1
  154.7 56.5 %layer_backward.2 = (f32[128,576]{1,0:T(8,128)}, f32[48,576]{1,0:T(8,128)}, bf16[576,128]{1,0:T(8,128)(2,1)}, bf16[3,128,128]{2,1,0:T(8,128)(2,1)}, bf16[128,576]{1,0:T(8,128)(2,1)}, /*index=5*/f32[8,576]{1,0:T(8,128)}) custom-call(f32[128,576]{1,0:T(8,128)} %get-tuple-element.126.refs_0_, f32[128,576]{1,0:T(8,128)} %copy-done.5, ...), custom_call_target="tpu_custom_call" | custom-call | tf_op jit(solution)/shard_map/layer_backward/pallas_call | solution.py:883
  211.3 57.1 %layer_backward.3 = (f32[128,576]{1,0:T(8,128)}, f32[48,576]{1,0:T(8,128)}, bf16[576,128]{1,0:T(8,128)(2,1)}, bf16[3,128,128]{2,1,0:T(8,128)(2,1)}, bf16[128,576]{1,0:T(8,128)(2,1)}, /*index=5*/f32[8,576]{1,0:T(8,128)}) custom-call(f32[128,576]{1,0:T(8,128)} %get-tuple-element.66.refs_0_, f32[128,576]{1,0:T(8,128)} %copy-done.1, ...), custom_call_target="tpu_custom_call" | custom-call | tf_op jit(solution)/shard_map/layer_backward/pallas_call | solution.py:883
  268.4 1.1 fusion.7
  269.5 1.0 fusion
  270.5 0.9 copy.39
  271.3 0.7 pad_maximum_fusion.3.gains
  272.1 0.9 copy-done.28
  273.0 0.9 copy-done.29
  273.9 0.9 copy-done.32
  274.8 26.6 %reduce_last.1 = (f32[48,576]{1,0:T(8,128)S(1)}, f32[16,576]{1,0:T(8,128)S(1)}) custom-call(bf16[576,128]{1,0:T(8,128)(2,1)S(1)} %copy-done.29, bf16[3,128,128]{2,1,0:T(8,128)(2,1)S(1)} %copy-done.32, bf16[576,128]{1,0:T(8,128)(2,1)S(1)} %copy-done.15, bf16[128,576]{1,0:T(8,128)(2,1)S(1)} %copy-done.12, bf16[128,576]{1,0:T(8,128)(2,1)S(1)} %copy-done.28, ...), custom_call_target="tpu_custom_call" | custom-call | tf_op jit(solution)/shard_map/reduce_last/pallas_call | solution.py:1195
  (93 shorter events, 10.7 us)
Async XLA Ops:
  0.6 38.3 %copy-start.39 = (s32[1,128]{1,0:T(1,128)S(1)}, s32[1,128]{1,0:T(1,128)}, u32[]{:S(2)}) copy-start(s32[1,128]{1,0:T(1,128)} %param.6) | copy-start | bytes 1540
  0.6 40.4 %copy-start.35 = (bf16[2,48,576]{2,1,0:T(8,128)(2,1)S(1)}, bf16[2,48,576]{2,1,0:T(8,128)(2,1)}, u32[]{:S(2)}) copy-start(bf16[2,48,576]{2,1,0:T(8,128)(2,1)} %param.7) | copy-start | bytes 331780
  6.3 138.7 %copy-start.1 = (f32[128,576]{1,0:T(8,128)}, f32[128,576]{1,0:T(8,128)S(1)}, u32[]{:S(2)}) copy-start(f32[128,576]{1,0:T(8,128)S(1)} %get-tuple-element.125.hidden.refs_1_) | copy-start | bytes 884740
  38.9 106.1 %copy-start.24 = (f32[8,576]{1,0:T(8,128)}, f32[8,576]{1,0:T(8,128)S(1)}, u32[]{:S(2)}) copy-start(f32[8,576]{1,0:T(8,128)S(1)} %get-tuple-element.117.gains.refs_4_) | copy-start | bytes 55300
  38.9 106.1 %copy-start.25 = (f32[8,576]{1,0:T(8,128)}, f32[8,576]{1,0:T(8,128)S(1)}, u32[]{:S(2)}) copy-start(f32[8,576]{1,0:T(8,128)S(1)} %get-tuple-element.116.gains.refs_4_) | copy-start | bytes 55300
  39.6 105.4 %copy-start.2 = (f32[128,128]{1,0:T(8,128)}, f32[128,128]{1,0:T(8,128)S(1)}, u32[]{:S(2)}) copy-start(f32[128,128]{1,0:T(8,128)S(1)} %get-tuple-element.127.cosine.refs_5_) | copy-start | bytes 196612
  39.6 105.4 %copy-start.3 = (f32[128,128]{1,0:T(8,128)}, f32[128,128]{1,0:T(8,128)S(1)}, u32[]{:S(2)}) copy-start(f32[128,128]{1,0:T(8,128)S(1)} %get-tuple-element.128.sine.refs_6_) | copy-start | bytes 196612
  40.9 104.1 %copy-start.4 = (f32[40,384]{1,0:T(8,128)}, f32[40,384]{1,0:T(8,128)S(1)}, u32[]{:S(2)}) copy-start(f32[40,384]{1,0:T(8,128)S(1)} %broadcast_in_dim.8.flags.refs_9_) | copy-start | bytes 184324
  41.0 104.0 %copy-start = (f32[40,8,128]{2,1,0:T(8,128)}, f32[40,8,128]{2,1,0:T(8,128)S(1)}, u32[]{:S(2)}) copy-start(f32[40,8,128]{2,1,0:T(8,128)S(1)} %broadcast_in_dim.9.tall.refs_10_) | copy-start | bytes 491524
  89.2 0.9 copy-start.6
  90.1 0.9 copy-start.7
  92.3 0.8 copy-start.16
  93.2 0.7 copy-start.18
  93.9 0.7 copy-start.20
  94.6 0.7 copy-start.22
  95.4 0.7 copy-start.26
  97.3 47.8 %copy-start.5 = (f32[128,576]{1,0:T(8,128)}, f32[128,576]{1,0:T(8,128)S(1)}, u32[]{:S(2)}) copy-start(f32[128,576]{1,0:T(8,128)S(1)} %get-tuple-element.50.hidden.refs_1_) | copy-start | bytes 884740
  145.1 0.9 copy-start.8
  146.0 0.9 copy-start.9
  146.9 0.7 copy-start.10
  148.2 0.8 copy-start.17
  149.0 0.8 copy-start.19
  149.8 0.7 copy-start.21
  150.5 0.7 copy-start.23
  211.3 60.1 %copy-start.38 = (f32[8,576]{1,0:T(8,128)S(1)}, f32[8,576]{1,0:T(8,128)}, u32[]{:S(2)}) copy-start(f32[8,576]{1,0:T(8,128)} %get-tuple-element.87) | copy-start | bytes 55300
  211.3 60.8 %copy-start.12 = (bf16[128,576]{1,0:T(8,128)(2,1)S(1)}, bf16[128,576]{1,0:T(8,128)(2,1)}, u32[]{:S(2)}) copy-start(bf16[128,576]{1,0:T(8,128)(2,1)} %copy-done.11) | copy-start | bytes 442372
  211.3 60.8 %copy-start.15 = (bf16[576,128]{1,0:T(8,128)(2,1)S(1)}, bf16[576,128]{1,0:T(8,128)(2,1)}, u32[]{:S(2)}) copy-start(bf16[576,128]{1,0:T(8,128)(2,1)} %copy-done.14) | copy-start | bytes 442372
  268.4 33.1 %copy-start.36 = (f32[48,576]{1,0:T(8,128)S(1)}, f32[48,576]{1,0:T(8,128)}, u32[]{:S(2)}) copy-start(f32[48,576]{1,0:T(8,128)} %get-tuple-element.90) | copy-start | bytes 331780
  268.4 33.1 %copy-start.37 = (f32[48,576]{1,0:T(8,128)S(1)}, f32[48,576]{1,0:T(8,128)}, u32[]{:S(2)}) copy-start(f32[48,576]{1,0:T(8,128)} %get-tuple-element.89) | copy-start | bytes 331780
  272.1 0.9 copy-start.28
  273.0 0.9 copy-start.29
  273.9 0.9 copy-start.32
  (8 other events, 5.1 us)
